TPU v7x, 32 devices: a whole 2x2x4 slice. The times are simulated.
32 devices in a mesh: seq: 4 (over z), fsdp: 8 (over y, x, core).
Axes of the slice: x: 2, y: 2, z: 4, core: 2. Of those that a mesh axis runs over, the one named last changes fastest.
Arguments:
- tokens: bfloat16 [4096, 1024], P(('fsdp', 'seq')), may hold values from -6 to 6
- cotangent: bfloat16 [4096, 1024], P(('fsdp', 'seq')), may hold values from -6 to 6
- doc_starts: int32 [8], replicated, may hold values from 0 to 4095, as said below
- variate_ids: int32 [4096], replicated, may hold values from 0 to 7, as said below
- time_ids: int32 [4096], replicated, may hold values from 0 to 63, as said below
- gain_attn: float32 [1024], replicated, may hold values from 0.5 to 1.5
- w_attn: bfloat16 [1024, 3072], P('fsdp'), may hold values from -0.1875 to 0.1875
- gain_query: float32 [64], replicated, may hold values from 0.5 to 1.5
- gain_key: float32 [64], replicated, may hold values from 0.5 to 1.5
- variate_bias: float32 [16, 2], replicated, may hold values from -3 to 3
- w_output: bfloat16 [1024, 1024], P('fsdp'), may hold values from -3 to 3
- gain_feed: float32 [1024], replicated, may hold values from 0.5 to 1.5
- w_gate: bfloat16 [1024, 4096], P('fsdp'), may hold values from -0.1875 to 0.1875
- w_up: bfloat16 [1024, 4096], P('fsdp'), may hold values from -0.1875 to 0.1875
- w_down: bfloat16 [4096, 1024], P('fsdp'), may hold values from -0.09375 to 0.09375
Outputs:
- layer_out: bfloat16 [4096, 1024], P(('fsdp', 'seq'))
- tokens_grad: float32 [4096, 1024], P(('fsdp', 'seq'))
- attn_grad: float32 [1024, 3072], P(('seq', 'fsdp'))
- output_grad: float32 [1024, 1024], P(('seq', 'fsdp'))
- gate_grad: float32 [1024, 4096], P(('seq', 'fsdp'))
- up_grad: float32 [1024, 4096], P(('seq', 'fsdp'))
- down_grad: float32 [4096, 1024], P(('seq', 'fsdp'))
- attn_gain_grad: float32 [1024], P(('seq', 'fsdp'))
- feed_gain_grad: float32 [1024], P(('seq', 'fsdp'))
- query_gain_grad: float32 [64], replicated
- key_gain_grad: float32 [64], replicated
- bias_grad: float32 [16, 2], replicated
Inputs may be any that keep to these rules, and one draw needn't show every extreme that they name: `doc_starts`: non-decreasing, the first entry is 0. `variate_ids`: only compared for equality within a document. `time_ids`: a time index modulo 64; token 0 has 63.
All inputs are finite; a program needn't handle non-finite values.
Results may differ from a plain program's by a relative error of at most 0.038.
Values may be sent and summed in bfloat16 or wider, within the bound.
A program may use at most 256 MiB of HBM per device.

v0:
```python
import functools

import jax
import jax.numpy as jnp
from jax import lax
from jax.experimental import pallas as pl
from jax.experimental.pallas import tpu as pltpu
from jax.sharding import PartitionSpec as P

EPSILON = 1e-06
F32, BF16 = jnp.float32, jnp.bfloat16
VARIATES = 8
AWAY = 1024.0
QUERY_BLOCK = 256
LSE_ROW, VAR_ROW = 32, 40
MESH = pl.DeviceIdType.MESH
ANY = pl.BlockSpec(memory_space=pl.ANY)
VMEM = pl.BlockSpec(memory_space=pltpu.VMEM)
VMEM_BYTES = 56 * 2**20


def nn(a, b):
    return jnp.dot(a, b, preferred_element_type=F32)


def nt(a, b):
    return lax.dot_general(a, b, (((1,), (1,)), ((), ())), preferred_element_type=F32)


def tn(a, b):
    return lax.dot_general(a, b, (((0,), (0,)), ((), ())), preferred_element_type=F32)


def pieces(values):
    high = values.astype(BF16).astype(F32)
    middle = (values - high).astype(BF16).astype(F32)
    return high, middle, (values - high - middle).astype(BF16).astype(F32)


def send_all(plan, send_sems, recv_sems, local_sems):
    remote, local = plan
    copies = []
    for n, (src, dst, device, may_send, may_receive) in enumerate(remote):
        copy = pltpu.make_async_remote_copy(
            src_ref=src,
            dst_ref=dst,
            send_sem=send_sems.at[n],
            recv_sem=recv_sems.at[n],
            device_id=device,
            device_id_type=MESH,
        )
        when(may_send, copy.start)
        copies.append((copy, may_send, may_receive))
    locals_ = []
    for n, (src, dst, may) in enumerate(local):
        copy = pltpu.make_async_copy(src, dst, local_sems.at[n])
        when(may, copy.start)
        locals_.append((copy, may))

    def finish():
        for copy, may in locals_:
            when(may, copy.wait)
        for copy, may_send, may_receive in copies:
            when(may_send, copy.wait_send)
            when(may_receive, copy.wait_recv)

    return finish


def when(condition, action):
    if condition is None:
        action()
    else:
        pl.when(condition)(action)


def greet(devices):
    barrier = pltpu.get_barrier_semaphore()
    for device in devices:
        pl.semaphore_signal(barrier, inc=1, device_id=device, device_id_type=MESH)
    pl.semaphore_wait(barrier, len(devices))


class Line:
    def __init__(self, block, sems, s, f, S):
        self.block, (self.sent, self.got) = block, sems
        self.s, self.f, self.S = s, f, S

    def hop(self, plane, slot, step):
        ref = self.block(plane, slot)
        return pltpu.make_async_remote_copy(
            src_ref=ref,
            dst_ref=ref,
            send_sem=self.sent.at[plane, slot, int(step > 0)],
            recv_sem=self.got.at[plane, slot],
            device_id=(self.s + step, self.f),
            device_id_type=MESH,
        )

    def each_hop(self, slot, distance, action):
        s, S = self.s, self.S
        pl.when((s - distance + 1) * (S - 1 - s) > 0)(
            lambda: action(self.hop(s - distance, slot, 1))
        )
        pl.when((S - s - distance) * s > 0)(lambda: action(self.hop(s + distance, slot, -1)))

    def send(self, slot):
        self.each_hop(slot, 0, lambda hop: hop.start())

    def arrive(self, slot, distance):
        s, S = self.s, self.S
        pl.when(s - distance >= 0)(lambda: self.hop(s - distance, slot, 1).wait_recv())
        pl.when(s + distance < S)(lambda: self.hop(s + distance, slot, -1).wait_recv())
        self.each_hop(slot, distance, lambda hop: hop.start())

    def drain(self, slot):
        for distance in range(self.S):
            self.each_hop(slot, distance, lambda hop: hop.wait_send())


def line_sems(S, slots):
    return [pltpu.SemaphoreType.DMA((S, slots, 2)), pltpu.SemaphoreType.DMA((S, slots))]


class LineSum:
    def __init__(self, terms, from_left, from_right, sems, s, f, S):
        self.terms, self.from_left, self.from_right = terms, from_left, from_right
        self.sent, self.got = sems
        self.s, self.f, self.S = s, f, S

    def hop(self, t, to_right):
        return pltpu.make_async_remote_copy(
            src_ref=self.terms.at[t],
            dst_ref=(self.from_left if to_right else self.from_right).at[t],
            send_sem=self.sent.at[int(to_right), t],
            recv_sem=self.got.at[int(to_right), t],
            device_id=(self.s + (1 if to_right else -1), self.f),
            device_id_type=MESH,
        )

    def take(self, t, to_right):
        self.hop(t, to_right).wait_recv()
        came = (self.from_left if to_right else self.from_right)[t]
        self.terms[t] = (self.terms[t].astype(F32) + came.astype(F32)).astype(BF16)

    def step(self, time):
        s, S = self.s, self.S
        n = time - s
        pl.when((n >= 0) & (s >= 1))(lambda: self.take(S - 1 - n, True))
        pl.when((n >= 0) & (S - 1 - n > s))(lambda: self.hop(S - 1 - n, True).start())
        m = time - (S - 1 - s)
        pl.when((m >= 0) & (s < S - 1))(lambda: self.take(m, False))
        pl.when((m >= 0) & (m < s))(lambda: self.hop(m, False).start())

    def drain(self):
        for t in range(self.S):
            pl.when(self.s < t)(lambda t=t: self.hop(t, True).wait_send())
            pl.when(self.s > t)(lambda t=t: self.hop(t, False).wait_send())


def flipped(f, bit):
    step = 2**bit
    return f + step - 2 * step * lax.rem(f // step, 2)


class CubeGather:
    def __init__(self, block, own, sems, s, f, F):
        self.block, self.own, (self.sent, self.shared, self.got) = block, own, sems
        self.s, self.f, self.F = s, f, F
        bits = list(range(1, F.bit_length() - 1))
        self.orders = (bits, bits[::-1])

    def copy(self, g, half, sem, to, own=False):
        ref = self.block(g, half)
        return pltpu.make_async_remote_copy(
            src_ref=self.own(half) if own else ref,
            dst_ref=ref,
            send_sem=sem,
            recv_sem=self.got.at[g, half],
            device_id=(self.s, to),
            device_id_type=MESH,
        )

    def held(self, half, rounds):
        masks = [((), 0)]
        for n, bit in enumerate(self.orders[half][:rounds]):
            masks += [(mask + (bit,), n + 1) for mask, _ in list(masks)]
        return masks

    def device(self, mask):
        g = self.f
        for bit in mask:
            g = flipped(g, bit)
        return g

    def sends(self, half, since):
        rounds = len(self.orders[half])
        out = []
        for place, (mask, came) in enumerate(self.held(half, rounds)):
            for n in range(came, rounds):
                if came == since:
                    out.append((n, place, mask))
        return out

    def send(self, half, n, place, mask):
        bit = self.orders[half][n]
        sem = self.sent.at[half, n, place]
        return self.copy(self.device(mask), half, sem, flipped(self.f, bit), not mask)

    def shares(self, half, since):
        return [
            self.copy(
                self.device(mask), half, self.shared.at[half, place], flipped(self.f, 0), not mask
            )
            for place, (mask, came) in enumerate(self.held(half, len(self.orders[half])))
            if came == since
        ]

    @property
    def rounds(self):
        return len(self.orders[0])

    def start(self):
        for half in range(2):
            self.send(half, 0, 0, ()).start()
        for half in range(2):
            self.shares(half, 0)[0].start()

    def step(self, number):
        for half in range(2):
            shares = self.shares(half, number)
            for share in shares:
                share.wait_recv()
            if number < self.rounds:
                for which in self.sends(half, number) + self.sends(half, 0)[number : number + 1]:
                    if which[0] == number or which[1]:
                        self.send(half, *which).start()
            for share in shares:
                share.start()

    def finish(self):
        for half in range(2):
            for place, (mask, _) in enumerate(self.held(half, self.rounds)):
                g = flipped(self.device(mask), 0)
                self.copy(g, half, self.shared.at[half, place], self.f).wait_recv()

    def drain(self):
        for half in range(2):
            for number in range(self.rounds + 1):
                for which in self.sends(half, number):
                    self.send(half, *which).wait_send()
                for share in self.shares(half, number):
                    share.wait_send()


def cube_sems(F):
    rounds = F.bit_length() - 2
    return [
        pltpu.SemaphoreType.DMA((2, rounds, F // 4)),
        pltpu.SemaphoreType.DMA((2, F // 2)),
        pltpu.SemaphoreType.DMA((F, 2)),
    ]


def shape(dims, dtype=BF16):
    return jax.ShapeDtypeStruct(tuple(dims), dtype)


def join(a, b):
    return jnp.concatenate([a, b], axis=0)


def side_by_side(ref, *index):
    return jnp.concatenate([ref[(*index, n)] for n in range(ref.shape[len(index)])], axis=1)


def forward_group(j, q_ref, kv_ref, qa_ref, ka_ref, att_ref, lse_ref, o_ref):
    width, rows = att_ref.shape[1:]
    span = q_ref.shape[-1]
    sub = QUERY_BLOCK // span

    def block(i, _):
        cols = pl.ds(pl.multiple_of(i * QUERY_BLOCK, QUERY_BLOCK), QUERY_BLOCK)
        q_t = jnp.concatenate([q_ref[j, i * sub + n] for n in range(sub)], axis=1)
        queries = join(q_t, qa_ref[j, :, cols]).T
        total = jnp.zeros((QUERY_BLOCK, 2 * width), F32)
        for g in range(kv_ref.shape[0]):
            kv = side_by_side(kv_ref, g)
            keys = join(kv[:width], ka_ref[g])
            values = join(kv[width:], jnp.ones((width, rows), BF16))
            weights = jnp.exp(nn(queries, keys)).astype(BF16)
            total += nt(weights, values)
        total = total.T
        weight_sum = total[width : width + 1]
        attended = total[:width] / weight_sum
        att_ref[j, :, cols] = attended
        o_ref[j, :, cols] = attended.astype(BF16)
        lse_ref[j, :, cols] = jnp.log(weight_sum)
        return 0

    lax.fori_loop(0, rows // QUERY_BLOCK, block, 0)


def with_rows(base, first, rows):
    index = lax.broadcasted_iota(jnp.int32, base.shape, 0)
    for n, row in enumerate(rows):
        base = jnp.where(index == first + n, row, base)
    return base


def backward_body(q_ref, kv_ref, qa_ref, ka_ref, do_ref, att_ref, lse_ref, dq_ref, dkv_ref, bias_ref, sum_ref):
    width, rows = att_ref.shape[1:]
    blocks = rows // QUERY_BLOCK
    span = q_ref.shape[-1]
    sub = QUERY_BLOCK // span
    sum_ref[...] = jnp.zeros_like(sum_ref)
    bias_ref[...] = jnp.zeros_like(bias_ref)

    def block(i, _):
        j = i // blocks
        first = (i % blocks) * sub
        cols = pl.ds(pl.multiple_of((i % blocks) * QUERY_BLOCK, QUERY_BLOCK), QUERY_BLOCK)
        q_t = jnp.concatenate([q_ref[j, first + n] for n in range(sub)], axis=1)
        marks = qa_ref[j, :, cols].astype(F32)
        extra = with_rows(marks, LSE_ROW, pieces(-lse_ref[j, :, cols])).astype(BF16)
        queries = join(q_t, extra).T
        grad_t = jnp.concatenate([do_ref[j, first + n] for n in range(sub)], axis=1)
        delta = jnp.sum(grad_t.astype(F32) * att_ref[j, :, cols], axis=0, keepdims=True)
        extra = with_rows(jnp.zeros((width, QUERY_BLOCK), F32), 0, pieces(-delta)).astype(BF16)
        grads = join(grad_t, extra).T
        query_sum = jnp.zeros((QUERY_BLOCK, 2 * width), F32)
        for g in range(kv_ref.shape[0]):
            kv = side_by_side(kv_ref, g)
            keys = join(kv[:width], ka_ref[g])
            values = join(kv[width:], jnp.ones((width, rows), BF16))
            probs = jnp.exp(nn(queries, keys))
            score_grad = (probs * nn(grads, values)).astype(BF16)
            sum_ref[g, width:, :] += nn(grad_t, probs.astype(BF16))
            sum_ref[g, :width, :] += nn(q_t, score_grad)
            query_sum += nt(score_grad, keys)
        query_sum = query_sum.T
        dq_ref[j, :, cols] = (query_sum[:width] * width**-0.5).astype(BF16)
        by_variate = query_sum[width : width + VARIATES]
        bias_ref[0] += by_variate * marks[VAR_ROW : VAR_ROW + VARIATES]
        bias_ref[1] += by_variate
        return 0

    lax.fori_loop(0, q_ref.shape[0] * blocks, block, 0)
    dkv_ref[...] = sum_ref[...].astype(BF16)


def rms_scale(vector, gain, axis=-1):
    return vector * lax.rsqrt(jnp.mean(vector * vector, axis=axis, keepdims=True) + EPSILON) * gain


def per_device(
    tokens,
    cotangent,
    doc_starts,
    variate_ids,
    time_ids,
    gain_attn,
    w_attn,
    gain_query,
    gain_key,
    variate_bias,
    w_output,
    gain_feed,
    w_gate,
    w_up,
    w_down,
):
    S, F = lax.axis_size("seq"), lax.axis_size("fsdp")
    s, f = lax.axis_index("seq"), lax.axis_index("fsdp")
    rows, width = tokens.shape
    heads = variate_bias.shape[0]
    dim = gain_query.shape[0]
    own_heads = heads // S
    splits = F // own_heads
    group = rows * S
    groups = F // splits
    hidden = w_down.shape[0] * F // S
    half = F // 2
    cut = width // (S * F)
    lanes = own_heads * dim

    def along_seq(s, f):
        return [(lax.rem(s + d, S), f) for d in range(1, S)]

    def along_fsdp(s, f):
        return [(s, lax.rem(f + d, F)) for d in range(1, F)]

    def along_both(s, f):
        return along_seq(s, f) + along_fsdp(s, f)

    def like_parts(s, f):
        return [
            (lax.rem(s + a, S), lax.rem(f + b * splits, F))
            for a in range(S)
            for b in range(groups)
            if a or b
        ]

    def everyone(s, f):
        return [(lax.rem(s + a, S), lax.rem(f + b, F)) for a in range(S) for b in range(F) if a or b]

    def seq_swap(s, f, src, dst):
        remote = [(src.at[t[0]], dst.at[s], t, None, None) for t in along_seq(s, f)]
        return remote, [(src.at[s], dst.at[s], None)]

    frequency = (10000.0 ** (-2.0 * jnp.arange(dim // 2, dtype=F32) / dim))[:, None]
    per_plane = F // S
    down_rows = w_down.shape[0] // S
    local_rows = w_attn.shape[0]
    total = F * group

    def peers_a(s, f):
        return [(lax.rem(s + 1, S), f), (lax.rem(s + S - 1, S), f)] + along_fsdp(s, f)

    def kernel_a(
        x_ref, w_ref, wo_ref, cot_ref, times_ref, freq_ref, gain_ref, gain_q_ref, gain_k_ref, ids_ref, ids_mine_ref,
        starts_ref, bias_ref,
        xs_ref, ws_ref, raw_ref, cots_ref, cos_ref, sin_ref, ka_ref, qa_ref, q_ref, kv_ref, wos_ref,
        q_out, kv_out, w_sem, x_sent, x_got, c_sent, c_got, pair_sent, pair_shared, pair_got,
        wo_sent, wo_shared, wo_got, kv_sent, kv_shared, kv_got, q_sent, q_got, own_sem,
    ):
        s, f = lax.axis_index("seq"), lax.axis_index("fsdp")
        loads = []
        for n in range(3):
            src = w_ref.at[:, pl.ds(pl.multiple_of(n * S * lanes + s * lanes, 128), lanes)]
            dst = ws_ref.at[pl.ds(f * local_rows, local_rows), pl.ds(n * lanes, lanes)]
            loads.append(pltpu.make_async_copy(src, dst, w_sem.at[n]))
        for load in loads:
            load.start()
        wo_here = pltpu.make_async_copy(wo_ref, wos_ref.at[pl.ds(f * local_rows, local_rows)], w_sem.at[3])
        wo_here.start()
        xs_ref[s] = x_ref[...]
        cots_ref[s] = cot_ref[...]
        greet(peers_a(s, f))
        xs = Line(lambda plane, slot: xs_ref.at[plane], (x_sent, x_got), s, f, S)
        xs.send(0)
        for load in loads:
            load.wait()

        def rows_of(ref):
            size = local_rows // 2
            return lambda g, half: ref.at[pl.ds(g * local_rows + half * size, size)]

        def half_of(ref):
            size = local_rows // 2
            return lambda half: ref.at[pl.ds(half * size, size)]

        ws = CubeGather(
            rows_of(ws_ref), lambda half: rows_of(ws_ref)(f, half), (pair_sent, pair_shared, pair_got), s, f, F
        )
        wos = CubeGather(rows_of(wos_ref), half_of(wo_ref), (wo_sent, wo_shared, wo_got), s, f, F)
        ws.start()

        angles = freq_ref[...] * times_ref[...].astype(F32)
        cos_ref[...] = jnp.cos(angles)
        sin_ref[...] = jnp.sin(angles)
        pair = [bias_ref[s * own_heads + f // splits, n] for n in range(2)]
        difference = pieces(jnp.full((VARIATES, group), pair[0] - pair[1], F32))
        index = lax.broadcasted_iota(jnp.int32, (VARIATES, group), 0)

        def marks(g, ids):
            positions = g * group + lax.broadcasted_iota(jnp.int32, (VARIATES, group), 1)
            docs = jnp.zeros((VARIATES, group), jnp.int32) - 1
            for n in range(doc_starts.shape[0]):
                docs = docs + (starts_ref[n] <= positions).astype(jnp.int32)
            return (docs == index).astype(F32), (ids == index).astype(F32)

        for g in range(F):
            doc, var = marks(g, ids_ref[g])
            tail = (index < 3).astype(F32)
            none = jnp.zeros((dim - LSE_ROW - VARIATES, group), F32)
            ka_ref[g] = jnp.concatenate([var, var, var, 1.0 - doc, tail, none]).astype(BF16)
        for j in range(groups):
            doc, var = marks(j * splits + lax.rem(f, splits), ids_mine_ref[j])
            none = jnp.zeros((VARIATES, group), F32)
            rest = jnp.zeros((dim - VAR_ROW - VARIATES, group), F32)
            scaled = [var * part for part in difference]
            qa_ref[j] = jnp.concatenate([*scaled, doc * -AWAY, none, var, rest]).astype(BF16)

        def kv_copy(g, b, src, sem, to):
            return pltpu.make_async_remote_copy(
                src_ref=src, dst_ref=kv_ref.at[g, b], send_sem=sem, recv_sem=kv_got.at[g, b],
                device_id=(s, to), device_id_type=MESH,
            )

        def to_heads(b, d):
            to = lax.rem(f + 2 * d, F)
            return kv_copy(f, b, kv_out.at[b, to // splits], kv_sent.at[b, d], to)

        def to_neighbour(b, d):
            g = lax.rem(f + 2 * d, F)
            src = kv_ref.at[g, b] if d else kv_out.at[b, f // splits]
            return kv_copy(g, b, src, kv_shared.at[b, d], flipped(f, 0))

        def queries_to_heads(b, d):
            to = lax.rem(f + d * splits, F)
            return pltpu.make_async_remote_copy(
                src_ref=q_out.at[b, to // splits], dst_ref=q_ref.at[f // splits, b], send_sem=q_sent.at[b, d],
                recv_sem=q_got.at[f // splits, b], device_id=(s, to), device_id_type=MESH,
            )

        def own_copies(b):
            return (
                pltpu.make_async_copy(kv_out.at[b, f // splits], kv_ref.at[f, b], own_sem.at[b, 0]),
                pltpu.make_async_copy(q_out.at[b, f // splits], q_ref.at[f // splits, b], own_sem.at[b, 1]),
            )

        def project(b):
            normed = rms_scale(xs_ref[b].astype(F32), gain_ref[...]).astype(BF16)
            projected = nn(normed, ws_ref[...]).T.reshape(3, own_heads, dim, rows)
            cols = pl.ds(pl.multiple_of(b * rows, rows), rows)
            cosine, sine = cos_ref[:, cols], sin_ref[:, cols]

            def turned(raw, gain):
                raw = rms_scale(raw, gain, axis=1)
                front, back = raw[:, : dim // 2], raw[:, dim // 2 :]
                return jnp.concatenate(
                    [front * cosine - back * sine, front * sine + back * cosine], axis=1
                )

            raw_ref[0, :, :, cols] = projected[0]
            raw_ref[1, :, :, cols] = projected[1]
            q_out[b] = (turned(projected[0], gain_q_ref[...]).astype(BF16).astype(F32) * dim**-0.5).astype(BF16)
            kv_out[b, :, :dim] = turned(projected[1], gain_k_ref[...]).astype(BF16)
            kv_out[b, :, dim:] = projected[2].astype(BF16)
            for d in range(1, half):
                to_heads(b, d).start()
            for d in range(1, groups):
                queries_to_heads(b, d).start()
            to_neighbour(b, 0).start()
            for copy in own_copies(b):
                copy.start()

        def share(b):
            for d in range(1, half):
                to_neighbour(b, d).wait_recv()
                to_neighbour(b, d).start()

        for number in range(1, ws.rounds + 1):
            ws.step(number)
        wos.start()
        ws.finish()
        project(s)
        cots = Line(lambda plane, slot: cots_ref.at[plane], (c_sent, c_got), s, f, S)
        for distance in range(1, S):
            xs.arrive(0, distance)
            if distance == min(2, S - 1):
                cots.send(0)
            pl.when(s - distance >= 0)(lambda distance=distance: project(s - distance))
            pl.when(s + distance < S)(lambda distance=distance: project(s + distance))
            if distance < S - 1 and distance < wos.rounds:
                wos.step(distance)

        def share_all(b, _):
            share(b)
            return 0

        lax.fori_loop(0, S, share_all, 0)
        for number in range(min(S - 1, wos.rounds), wos.rounds + 1):
            wos.step(number)
        for distance in range(1, S):
            cots.arrive(0, distance)

        def last(b, _):
            for copy in own_copies(b):
                copy.wait()
            for d in range(half):
                if d:
                    to_heads(b, d).wait_send()
                to_neighbour(b, d).wait_send()
                g = lax.rem(flipped(f, 0) + 2 * d, F)
                kv_copy(g, b, kv_ref.at[g, b], kv_shared.at[b, d], f).wait_recv()
            for d in range(1, groups):
                queries_to_heads(b, d).wait_send()
                g = lax.rem(f + d * splits, F)
                pltpu.make_async_remote_copy(
                    src_ref=q_out.at[b, 0], dst_ref=q_ref.at[g // splits, b], send_sem=q_sent.at[b, d],
                    recv_sem=q_got.at[g // splits, b], device_id=(s, g), device_id_type=MESH,
                ).wait_recv()
            return 0

        lax.fori_loop(0, S, last, 0)
        for line in (xs, cots):
            line.drain(0)
        wos.finish()
        wo_here.wait()
        ws.drain()
        wos.drain()

    smem = pl.BlockSpec(memory_space=pltpu.SMEM)
    ids = variate_ids.reshape(F, 1, group)
    ids_mine = lax.dynamic_index_in_dim(
        ids.reshape(groups, splits, 1, group), lax.rem(f, splits), 1, keepdims=False
    )
    x_parts, w_qkv, raw, cot_parts, cosine, sine, key_marks, query_marks, q_all, kv_all, output_full = pl.pallas_call(
        kernel_a,
        in_specs=[VMEM, ANY, ANY] + [VMEM] * 8 + [smem] * 2,
        out_specs=[VMEM] * 8 + [ANY] * 3,
        out_shape=[
            shape((S, rows, width)),
            shape((width, 3 * lanes)),
            shape((2, own_heads, dim, group), F32),
            shape((S, rows, width)),
            shape((dim // 2, group), F32),
            shape((dim // 2, group), F32),
            shape((F, dim, group)),
            shape((groups, dim, group)),
            shape((groups, S, dim, rows)),
            shape((F, S, 2 * dim, rows)),
            shape((heads * dim, width)),
        ],
        scratch_shapes=[
            pltpu.VMEM((S, own_heads, dim, rows), BF16),
            pltpu.VMEM((S, own_heads, 2 * dim, rows), BF16),
            pltpu.SemaphoreType.DMA((4,)),
            *line_sems(S, 1),
            *line_sems(S, 1),
            *cube_sems(F),
            *cube_sems(F),
            pltpu.SemaphoreType.DMA((S, half)),
            pltpu.SemaphoreType.DMA((S, half)),
            pltpu.SemaphoreType.DMA((F, S)),
            pltpu.SemaphoreType.DMA((S, groups)),
            pltpu.SemaphoreType.DMA((groups, S)),
            pltpu.SemaphoreType.DMA((S, 2)),
        ],
        compiler_params=pltpu.CompilerParams(
            collective_id=0, has_side_effects=True, vmem_limit_bytes=VMEM_BYTES
        ),
        cost_estimate=pl.CostEstimate(flops=10**9, bytes_accessed=10**8, transcendentals=0),
    )(
        tokens,
        w_attn,
        w_output,
        cotangent,
        lax.dynamic_slice_in_dim(time_ids, f * group, group)[None, :],
        frequency,
        gain_attn[None, :],
        gain_query[:, None],
        gain_key[:, None],
        ids,
        ids_mine,
        doc_starts,
        variate_bias,
    )
    head = s * own_heads + f // splits

    def unit_place(s, f):
        return lax.rem(f, per_plane) * S + lax.rem(f // per_plane + s, S)

    def unit_block(s, g):
        holder = lax.rem(lax.rem(g, S) - s + S, S) * per_plane + g // S
        return holder * S + lax.rem(g, S)

    def units(w):
        if down_rows % 128 == 0:
            return w
        blocks = w.reshape(w.shape[0], S * F, down_rows)
        return jnp.concatenate(
            [lax.dynamic_index_in_dim(blocks, unit_block(s, g), 1, False) for g in range(F)], axis=1
        )

    def kernel_b(
        q_ref, kv_ref, qa_ref, ka_ref, wd_ref, wg_ref, wu_ref,
        att_ref, lse_ref, heads_ref, downs_ref, gates_ref, ups_ref,
        o_ref, gate_own, up_own, o_sent, h_sent, h_got, w_sem, here_sem, *cube_refs,
    ):
        s, f = lax.axis_index("seq"), lax.axis_index("fsdp")
        column, part = f // splits, lax.rem(f, splits)
        down_own = wd_ref.at[lax.rem(f // per_plane + s, S)]
        loads = []
        for n, (src, dst) in enumerate(((wg_ref, gate_own), (wu_ref, up_own))):
            if down_rows % 128:
                loads.append(pltpu.make_async_copy(src, dst, w_sem.at[n, 0]))
                continue
            for g in range(F):
                cols = pl.ds(pl.multiple_of(unit_block(s, g) * down_rows, 128), down_rows)
                place = pl.ds(g * down_rows, down_rows)
                loads.append(pltpu.make_async_copy(src.at[:, cols], dst.at[:, place], w_sem.at[n, g]))
        for load in loads:
            load.start()
        greet(along_both(s, f))
        for load in loads:
            load.wait()
        mine = pl.ds(f * local_rows, local_rows)
        here = [
            pltpu.make_async_copy(gate_own, gates_ref.at[mine], here_sem.at[0]),
            pltpu.make_async_copy(up_own, ups_ref.at[mine], here_sem.at[1]),
            pltpu.make_async_copy(
                down_own, downs_ref.at[pl.ds(unit_place(s, f) * down_rows, down_rows)], here_sem.at[2]
            ),
        ]
        for copy in here:
            copy.start()

        def rows_of(ref, size, place=lambda g: g):
            return lambda g, half: ref.at[pl.ds(place(g) * size + half * (size // 2), size // 2)]

        def half_of(ref, size):
            return lambda half: ref.at[pl.ds(half * (size // 2), size // 2)]

        blocks = (
            (rows_of(gates_ref, local_rows), half_of(gate_own, local_rows)),
            (rows_of(ups_ref, local_rows), half_of(up_own, local_rows)),
            (rows_of(downs_ref, down_rows, lambda g: unit_place(s, g)), half_of(down_own, down_rows)),
        )
        gathers = [
            CubeGather(block, mine, cube_refs[3 * n : 3 * n + 3], s, f, F)
            for n, (block, mine) in enumerate(blocks)
        ]
        for gather in gathers:
            gather.start()

        own = s * own_heads + column

        def to_column(turn):
            j = lax.rem(column + turn, groups)
            return pltpu.make_async_remote_copy(
                src_ref=o_ref.at[j], dst_ref=heads_ref.at[own], send_sem=o_sent.at[turn], recv_sem=h_got.at[turn, 0],
                device_id=(s, j * splits + part), device_id_type=MESH,
            )

        def along(turn, d):
            ref = heads_ref.at[s * own_heads + lax.rem(column - turn + groups, groups)]
            return pltpu.make_async_remote_copy(
                src_ref=ref, dst_ref=ref, send_sem=h_sent.at[turn, d], recv_sem=h_got.at[turn, d],
                device_id=(lax.rem(s + d, S), f), device_id_type=MESH,
            )

        for turn in range(groups + 1):
            if turn < groups:
                j = lax.rem(column + turn, groups)
                forward_group(j, q_ref, kv_ref, qa_ref, ka_ref, att_ref, lse_ref, o_ref)
                if turn:
                    to_column(turn).start()
                else:
                    heads_ref[own] = o_ref[j]
            if turn != 1:
                came = max(turn - 1, 0)
                if came:
                    to_column(came).wait_recv()
                for d in range(1, S):
                    along(came, d).start()
        for number in range(1, gathers[0].rounds + 1):
            for gather in gathers:
                gather.step(number)
        for turn in range(groups):
            if turn:
                to_column(turn).wait_send()
            for d in range(1, S):
                along(turn, d).wait()
        for copy in here:
            copy.wait()
        for gather in gathers:
            gather.finish()
            gather.drain()

    attended, log_sum, heads_t, down_full, gate_full, up_full = pl.pallas_call(
        kernel_b,
        in_specs=[VMEM] * 4 + [ANY] * 3,
        out_specs=[VMEM] * 3 + [ANY] * 3,
        out_shape=[
            shape((groups, dim, group), F32),
            shape((groups, 1, group), F32),
            shape((heads, dim, group)),
            shape((hidden, width)),
            shape((width, hidden)),
            shape((width, hidden)),
        ],
        scratch_shapes=[
            pltpu.VMEM((groups, dim, group), BF16),
            pltpu.VMEM((local_rows, hidden), BF16),
            pltpu.VMEM((local_rows, hidden), BF16),
            pltpu.SemaphoreType.DMA((groups,)),
            *[pltpu.SemaphoreType.DMA((groups, S))] * 2,
            pltpu.SemaphoreType.DMA((2, F)),
            pltpu.SemaphoreType.DMA((3,)),
            *cube_sems(F),
            *cube_sems(F),
            *cube_sems(F),
        ],
        compiler_params=pltpu.CompilerParams(
            collective_id=1, has_side_effects=True, vmem_limit_bytes=VMEM_BYTES
        ),
        cost_estimate=pl.CostEstimate(flops=2 * 10**10, bytes_accessed=10**8, transcendentals=10**7),
    )(
        q_all, kv_all, query_marks, key_marks, w_down.reshape(S, down_rows, width), units(w_gate), units(w_up)
    )
    heads_t = heads_t.reshape(heads * dim, group)

    def pair(s, f):
        return (s, flipped(f, 0))

    def same_parity(s, f):
        return [(s, lax.rem(f + 2 * d, F)) for d in range(1, half)]

    def peers_c(s, f):
        return like_parts(s, f) + [(s, lax.rem(f + d, F)) for d in range(1, F) if d % splits]

    block = 256 if width % 256 == 0 and hidden % 256 == 0 else 128

    def kernel_c(
        heads_ref, wo_ref, xs_ref, wg_ref, wu_ref, cots_ref, wd_ref, gain_ref,
        grads_ref, middle_ref, mid_grad_ref, feed_ref, out_ref, gate_got, up_got, down_half, output_half,
        h_v, wo_v, x_v, wg_v, wu_v, cot_v, wd_v, mid_v, n_v, n_t, hid_v, hid_t, gl_v, ul_v, u_ref, from_left, from_right,
        gate_part, up_part, down_part, output_part, gate_other, up_other, down_other, output_other, gate_half, up_half,
        hg_ref, load_sem, u_sent, u_got, pair_sent, pair_got, spread_sent, spread_got, own_sem, f_sent, f_got,
    ):
        s, f = lax.axis_index("seq"), lax.axis_index("fsdp")
        loads = [
            pltpu.make_async_copy(src, dst, load_sem.at[n])
            for n, (src, dst) in enumerate(
                (
                    (heads_ref, h_v), (wo_ref, wo_v), (xs_ref, x_v), (wg_ref, wg_v), (wu_ref, wu_v), (cots_ref, cot_v),
                    (wd_ref, wd_v),
                )
            )
        ]
        for load in loads:
            load.start()
        greet(peers_c(s, f))

        def copy(src, dst, sent, got, to):
            return pltpu.make_async_remote_copy(
                src_ref=src, dst_ref=dst, send_sem=sent, recv_sem=got, device_id=to, device_id_type=MESH
            )

        for load in loads[:3]:
            load.wait()
        heads_rows = h_v[...].T
        for c in range(0, width, block):
            cs = slice(c, c + block)
            mid_v[:, cs] = x_v[:, cs].astype(F32) + nn(heads_rows, wo_v[:, cs])
        normed = rms_scale(mid_v[...], gain_ref[...]).astype(BF16)
        n_v[...] = normed
        n_t[...] = normed.T
        for load in loads[3:]:
            load.wait()
        for c in range(0, hidden, block):
            cs = slice(c, c + block)
            gate_act, up_act = nn(n_v[...], wg_v[:, cs]), nn(n_v[...], wu_v[:, cs])
            hidden_grad = nt(cot_v[...], wd_v[cs, :])
            sigmoid = jax.nn.sigmoid(gate_act)
            silu = gate_act * sigmoid
            hidden_low = (silu * up_act).astype(BF16)
            hid_v[:, cs] = hidden_low
            hid_t[cs, :] = hidden_low.T
            gl_v[:, cs] = (hidden_grad * up_act * sigmoid * (1.0 + gate_act * (1.0 - sigmoid))).astype(BF16)
            ul_v[:, cs] = (hidden_grad * silu).astype(BF16)
        for c in range(0, width, block):
            cs = slice(c, c + block)
            grad = nt(gl_v[...], wg_v[cs, :]) + nt(ul_v[...], wu_v[cs, :])
            u_ref[:, :, cs] = grad.astype(BF16).reshape(S, rows, block)
        mid_sum = LineSum(u_ref, from_left, from_right, (u_sent, u_got), s, f, S)
        mid_sum.step(0)

        parity = lax.rem(f, 2)
        by_owner = (S, half, 2, cut, block)

        def exchange_halves(n, part, other):
            away = part.at[:, 1 - parity] if len(part.shape) == 4 else part.at[:, :, 1 - parity]
            send = copy(away, other, pair_sent.at[n], pair_got.at[n], pair(s, f))
            send.start()
            return send

        for c in range(0, hidden, block):
            cs = slice(c, c + block)
            gate_part[..., cs] = nn(n_t[...], gl_v[:, cs]).astype(BF16).reshape(by_owner)
        swaps = [exchange_halves(0, gate_part, gate_other)]
        for c in range(0, hidden, block):
            cs = slice(c, c + block)
            up_part[..., cs] = nn(n_t[...], ul_v[:, cs]).astype(BF16).reshape(by_owner)
        swaps.append(exchange_halves(1, up_part, up_other))
        for c in range(0, width, block):
            cs = slice(c, c + block)
            down_part[..., cs] = nn(hid_t[...], cot_v[:, cs]).astype(BF16).reshape(half, 2, down_rows, block)
        swaps.append(exchange_halves(2, down_part, down_other))
        for c in range(0, width, block):
            cs = slice(c, c + block)
            out_ref[:, :, cs] = nn(hid_v[...], wd_v[:, cs]).astype(BF16).reshape(S, rows, block)

        def spread(n, halves, got):
            here = pltpu.make_async_copy(halves.at[:, f // 2], got.at[f // 2], own_sem.at[n])
            here.start()
            sends = []
            for d, to in enumerate(same_parity(s, f)):
                send = copy(halves.at[:, to[1] // 2], got.at[f // 2], spread_sent.at[n, d], spread_got.at[n, d], to)
                send.start()
                sends.append(send)
            return here, sends

        def add(a, b):
            return (a.astype(F32) + b.astype(F32)).astype(BF16)

        swaps[0].wait_recv()
        gate_half[...] = add(gate_part[:, :, parity], gate_other[...])
        spreads = [spread(0, gate_half, gate_got)]
        mid_sum.step(1)
        swaps[1].wait_recv()
        up_half[...] = add(up_part[:, :, parity], up_other[...])
        spreads.append(spread(1, up_half, up_got))
        swaps[2].wait_recv()
        down_half[...] = add(down_part[:, parity], down_other[...])
        for time in range(2, S):
            mid_sum.step(time)

        middle = mid_v[pl.ds(pl.multiple_of(s * rows, rows), rows), :]
        grad = u_ref[s].astype(F32)
        inverse = lax.rsqrt(jnp.mean(middle * middle, axis=1, keepdims=True) + EPSILON)
        scaled = grad * gain_ref[...]
        mean = jnp.mean(scaled * middle, axis=1, keepdims=True)
        own_cot = cot_v[pl.ds(pl.multiple_of(s * rows, rows), rows), :].astype(F32)
        middle_grad = own_cot + inverse * scaled - middle * (inverse**3 * mean)
        middle_low = middle_grad.astype(BF16)
        hg_ref[...] = nt(wo_v[...], middle_low).astype(BF16).reshape(heads, dim, rows)

        place = grads_ref.at[f // splits, s]
        grads_here = pltpu.make_async_copy(hg_ref.at[s * own_heads + f // splits], place, own_sem.at[2])
        grads_here.start()
        sends = []
        for n, to in enumerate(like_parts(s, f)):
            send = copy(hg_ref.at[to[0] * own_heads + to[1] // splits], place, f_sent.at[n], f_got.at[n], to)
            send.start()
            sends.append(send)

        middle_ref[...] = middle
        mid_grad_ref[...] = middle_grad
        feed_ref[...] = jnp.sum(grad * middle * inverse, axis=0, keepdims=True)
        own_heads_t = h_v[:, pl.ds(pl.multiple_of(s * rows, rows), rows)]
        for c in range(0, width, block):
            cs = slice(c, c + block)
            output_part[..., cs] = nn(own_heads_t, middle_low[:, cs]).astype(BF16).reshape(by_owner)
        swaps.append(exchange_halves(3, output_part, output_other))
        swaps[3].wait_recv()
        output_half[...] = add(output_part[:, :, parity], output_other[...])
        grads_here.wait()
        for send in sends:
            send.wait()
        for here, others in spreads:
            here.wait()
            for send in others:
                send.wait()
        for swap in swaps:
            swap.wait_send()
        mid_sum.drain()

    dma = pltpu.SemaphoreType.DMA
    wide = (S, half, 2, cut, hidden)
    wide_half = (S, half, cut, hidden)
    grad_heads, own_middle, middle_grad, feed_gain, out_part, gate_got, up_got, down_half, output_half = pl.pallas_call(
        kernel_c,
        in_specs=[ANY] * 7 + [VMEM],
        out_specs=[ANY] + [VMEM] * 4 + [ANY] * 2 + [VMEM] * 2,
        out_shape=[
            shape((groups, S, dim, rows)),
            shape((rows, width), F32),
            shape((rows, width), F32),
            shape((1, width), F32),
            shape((S, rows, width)),
            shape((half, S, cut, hidden)),
            shape((half, S, cut, hidden)),
            shape((half, down_rows, width)),
            shape((S, half, cut, width)),
        ],
        scratch_shapes=[
            pltpu.VMEM((heads * dim, group), BF16),
            pltpu.VMEM((heads * dim, width), BF16),
            pltpu.VMEM((group, width), BF16),
            pltpu.VMEM((width, hidden), BF16),
            pltpu.VMEM((width, hidden), BF16),
            pltpu.VMEM((group, width), BF16),
            pltpu.VMEM((hidden, width), BF16),
            pltpu.VMEM((group, width), F32),
            pltpu.VMEM((group, width), BF16),
            pltpu.VMEM((width, group), BF16),
            pltpu.VMEM((group, hidden), BF16),
            pltpu.VMEM((hidden, group), BF16),
            pltpu.VMEM((group, hidden), BF16),
            pltpu.VMEM((group, hidden), BF16),
            *[pltpu.VMEM((S, rows, width), BF16)] * 3,
            *[pltpu.VMEM(wide, BF16)] * 2,
            pltpu.VMEM((half, 2, down_rows, width), BF16),
            pltpu.VMEM((S, half, 2, cut, width), BF16),
            *[pltpu.VMEM(wide_half, BF16)] * 2,
            pltpu.VMEM((half, down_rows, width), BF16),
            pltpu.VMEM((S, half, cut, width), BF16),
            *[pltpu.VMEM(wide_half, BF16)] * 2,
            pltpu.VMEM((heads, dim, rows), BF16),
            dma((7,)),
            *[dma((2, S))] * 2,
            *[dma((4,))] * 2,
            *[dma((2, half))] * 2,
            dma((3,)),
            *[dma((S * groups,))] * 2,
        ],
        compiler_params=pltpu.CompilerParams(
            collective_id=2, has_side_effects=True, vmem_limit_bytes=VMEM_BYTES
        ),
        cost_estimate=pl.CostEstimate(flops=10**10, bytes_accessed=10**8, transcendentals=10**6),
    )(
        heads_t,
        output_full,
        x_parts.reshape(group, width),
        gate_full,
        up_full,
        cot_parts.reshape(group, width),
        down_full,
        gain_feed[None, :],
    )

    def kernel_g(*refs):
        ins, sends, outs, gots = refs[:7], refs[7:10], refs[10:13], refs[13:16]
        sum_ref, send_sems, recv_sems, local_sems = refs[16:]
        s, f = lax.axis_index("seq"), lax.axis_index("fsdp")
        greet(along_seq(s, f) + same_parity(s, f))
        remote, local = seq_swap(s, f, sends[2], gots[2])
        for t in same_parity(s, f):
            remote.append((sends[0].at[:, t[1] // 2], gots[0].at[f // 2], t, None, None))
            remote.append((sends[1].at[t[1] // 2], gots[1].at[f // 2], t, None, None))
        local.append((sends[0].at[:, f // 2], gots[0].at[f // 2], None))
        local.append((sends[1].at[f // 2], gots[1].at[f // 2], None))
        finish = send_all((remote, local), send_sems, recv_sems, local_sems)
        backward_body(*ins, *outs, sum_ref)
        finish()

    copies = S - 1 + 2 * (half - 1)
    query_grad, kv_grad, bias_terms, output_got, down_got, out_terms = pl.pallas_call(
        kernel_g,
        in_specs=[VMEM] * 7 + [ANY] * 3,
        out_specs=[VMEM] * 3 + [ANY] * 3,
        out_shape=[
            shape((groups, dim, group)),
            shape((F, 2 * dim, group)),
            shape((2, VARIATES, QUERY_BLOCK), F32),
            shape((half, S, cut, width)),
            shape((half, down_rows, width)),
            shape((S, rows, width)),
        ],
        scratch_shapes=[
            pltpu.VMEM((F, 2 * dim, group), F32),
            dma((copies,)),
            dma((copies,)),
            dma((3,)),
        ],
        compiler_params=pltpu.CompilerParams(
            collective_id=3, has_side_effects=True, vmem_limit_bytes=VMEM_BYTES
        ),
    )(
        q_all,
        kv_all,
        query_marks,
        key_marks,
        grad_heads,
        attended,
        log_sum,
        output_half,
        down_half,
        out_part,
    )

    bias_sums = jnp.sum(bias_terms, axis=(1, 2))
    bias_pair = jnp.stack([bias_sums[0], bias_sums[1] - bias_sums[0]])
    bias_row = lax.dynamic_update_slice_in_dim(jnp.zeros((heads, 2), F32), bias_pair[None], head, 0)
    bias_row = jnp.pad(bias_row.reshape(1, 2 * heads), ((0, 0), (0, 128 - 2 * heads)))
    count = S * F
    chunks = width // 128

    def kernel_h(
        dq_ref, dkv_ref, gate_got, up_got, out_got, down_got, out_terms, middle_ref, mid_grad_ref, raw_ref, cos_ref,
        sin_ref, gain_q_ref, gain_k_ref, gain_ref, ws_ref, xs_ref, feed_ref, bias_ref,
        layer_ref, tokens_ref, attn_ref, output_ref, gate_ref, up_ref, down_ref, sums_ref,
        dqs, dkvs, gate_sum, up_sum, out_sum, gate_rows, up_rows, out_rows, down_sum, down_rows_ref, down_sent, down_arrived, pg_ref, u_ref, from_left, from_right,
        w_part, w_got, w_sum, w_rows, vec, vec_got,
        dq_sent, dq_got, dkv_sent, dkv_got, own_sem, swap_sent, swap_got, u_sent, u_got,
        w_sent, w_arrived, rows_sent, rows_got, vec_sent, vec_arrived,
    ):
        s, f = lax.axis_index("seq"), lax.axis_index("fsdp")
        own = f // splits

        def copy(src, dst, sent, got, to):
            return pltpu.make_async_remote_copy(
                src_ref=src, dst_ref=dst, send_sem=sent, recv_sem=got, device_id=to, device_id_type=MESH
            )

        greet(everyone(s, f))
        pending = []
        here = [
            pltpu.make_async_copy(dkv_ref.at[f], dkvs.at[f], own_sem.at[0]),
            pltpu.make_async_copy(dq_ref.at[own], dqs.at[own], own_sem.at[1]),
        ]
        for load in here:
            load.start()
        for d in range(1, F):
            to, source = lax.rem(f + d, F), lax.rem(f + F - d, F)
            if d % splits == 0:
                send = copy(dq_ref.at[to // splits], dqs.at[own], dq_sent.at[d // splits], dq_got.at[d // splits], (s, to))
                send.start()
                pending.append(send)
            send = copy(dkv_ref.at[to], dkvs.at[f], dkv_sent.at[d], dkv_got.at[d], (s, to))
            send.start()
            pending.append(send)

        swaps = []
        for n, (got, total, rows_ref) in enumerate(
            ((gate_got, gate_sum, gate_rows), (up_got, up_sum, up_rows), (out_got, out_sum, out_rows))
        ):
            total[...] = jnp.sum(got[...].astype(F32), axis=0).astype(BF16)
            rows_ref[s] = total[s]
            for d in range(1, S):
                to = lax.rem(s + d, S)
                send = copy(total.at[to], rows_ref.at[s], swap_sent.at[n, d], swap_got.at[n, d], (to, f))
                send.start()
                swaps.append(send)
        layer_ref[...] = (middle_ref[...] + jnp.sum(out_terms[...].astype(F32), axis=0)).astype(BF16)
        to_plane = lax.rem(lax.rem(f, S) - s + S, S)
        down_sum[...] = jnp.sum(down_got[...].astype(F32), axis=0).astype(BF16)
        down_move = copy(down_sum, down_rows_ref, down_sent, down_arrived, (to_plane, f))
        pl.when(to_plane != s)(down_move.start)

        for load in here:
            load.wait()
        for send in pending:
            send.wait_recv()

        cosine, sine = cos_ref[...], sin_ref[...]

        def prepare_back(grad, raw, gain):
            front, back = grad[: dim // 2], grad[dim // 2 :]
            grad = join(front * cosine + back * sine, back * cosine - front * sine)
            inverse = lax.rsqrt(jnp.mean(raw * raw, axis=0, keepdims=True) + EPSILON)
            scaled = grad * gain
            mean = jnp.mean(scaled * raw, axis=0, keepdims=True)
            return inverse * scaled - raw * (inverse**3 * mean), grad * raw * inverse

        def gain_row(terms):
            folded = terms[:, :128]
            for n in range(1, group // 128):
                folded = folded + terms[:, n * 128 : (n + 1) * 128]
            return jnp.sum(folded.T, axis=0, keepdims=True)

        gain_terms = [jnp.zeros((dim, group), F32), jnp.zeros((dim, group), F32)]
        for h in range(own_heads):
            kv_sum = dkvs[h * splits].astype(F32)
            for n in range(1, splits):
                kv_sum = kv_sum + dkvs[h * splits + n].astype(F32)
            kv_sum = kv_sum.astype(BF16).astype(F32)
            for n, (grad, gain) in enumerate(
                ((dqs[h].astype(F32), gain_q_ref[...]), (kv_sum[:dim], gain_k_ref[...]))
            ):
                back, terms = prepare_back(grad, raw_ref[n, h], gain)
                gain_terms[n] += terms
                pg_ref[:, pl.ds(n * lanes + h * dim, dim)] = back.T.astype(BF16)
            pg_ref[:, pl.ds(2 * lanes + h * dim, dim)] = kv_sum[dim:].T.astype(BF16)

        attn_gain = jnp.zeros((1, width), F32)
        for b in range(S):
            grad = nt(pg_ref[pl.ds(b * rows, rows), :], ws_ref[...])
            x = xs_ref[b].astype(F32)
            inverse = lax.rsqrt(jnp.mean(x * x, axis=1, keepdims=True) + EPSILON)
            attn_gain += jnp.sum(grad * x * inverse, axis=0, keepdims=True)
            u_ref[b] = grad.astype(BF16)

        normed_sum = LineSum(u_ref, from_left, from_right, (u_sent, u_got), s, f, S)
        normed_sum.step(0)

        gains = jnp.concatenate([gain_row(gain_terms[0]), gain_row(gain_terms[1])], axis=1)
        gains = jnp.concatenate([gains, jnp.zeros((1, 256 - 2 * dim), F32)], axis=1)[:, :128]
        for n in range(chunks):
            part = slice(n * 128, (n + 1) * 128)
            vec[n] = jnp.concatenate(
                [attn_gain[:, part], feed_ref[:, part], gains, bias_ref[...], jnp.zeros((4, 128), F32)]
            )
        me = s * F + f
        vec_got[me] = vec[me * cut // 128]
        small = []
        for a in range(S):
            for b in range(F):
                if a or b:
                    to = (lax.rem(s + a, S), lax.rem(f + b, F))
                    chunk = (to[0] * F + to[1]) * cut // 128
                    small.append(
                        copy(vec.at[chunk], vec_got.at[me], vec_sent.at[a * F + b], vec_arrived.at[a * F + b], to)
                    )
                    small[-1].start()

        for b in range(S):
            normed = rms_scale(xs_ref[b].astype(F32), gain_ref[...]).astype(BF16)
            u_terms = tn(normed, pg_ref[pl.ds(b * rows, rows), :])
            if b == 0:
                total = u_terms
            else:
                total = total + u_terms
        w_part[...] = total.astype(BF16).reshape(S, F, cut, 3 * lanes)
        w_got[f] = w_part[:, f]
        for d in range(1, F):
            to = lax.rem(f + d, F)
            send = copy(w_part.at[:, to], w_got.at[f], w_sent.at[d], w_arrived.at[d], (s, to))
            send.start()
            swaps.append(send)
        attn_sends = swaps[-(F - 1) :]
        for n in range(1, S - 1):
            normed_sum.step(n)
        for send in attn_sends:
            send.wait_recv()
        w_sum[...] = jnp.sum(w_got[...].astype(F32), axis=0).astype(BF16)
        w_rows[s] = w_sum[s]
        last = []
        for d in range(1, S):
            to = lax.rem(s + d, S)
            last.append(copy(w_sum.at[to], w_rows.at[s], rows_sent.at[d], rows_got.at[d], (to, f)))
            last[-1].start()

        for send in swaps[: 3 * (S - 1)]:
            send.wait_recv()
        for n in range(S):
            for g in range(F):
                holder = (g % S - n) % S * per_plane + g // S
                place = (holder * S + g % S) * down_rows
                part = slice(g * down_rows, (g + 1) * down_rows)
                gate_ref[:, place : place + down_rows] = gate_rows[n, :, part].astype(F32)
                up_ref[:, place : place + down_rows] = up_rows[n, :, part].astype(F32)
        output_ref[...] = jnp.sum(out_rows[...].astype(F32), axis=0)
        pl.when(to_plane != s)(down_move.wait)

        @pl.when(to_plane != s)
        def _():
            down_ref[...] = down_rows_ref[...].astype(F32)

        @pl.when(to_plane == s)
        def _():
            down_ref[...] = down_sum[...].astype(F32)

        for send in small:
            send.wait_recv()
        sums_ref[...] = jnp.sum(vec_got[...], axis=0)

        normed_sum.step(S - 1)
        grad = u_ref[s].astype(F32)
        x = xs_ref[s].astype(F32)
        inverse = lax.rsqrt(jnp.mean(x * x, axis=1, keepdims=True) + EPSILON)
        scaled = grad * gain_ref[...]
        mean = jnp.mean(scaled * x, axis=1, keepdims=True)
        tokens_ref[...] = mid_grad_ref[...] + inverse * scaled - x * (inverse**3 * mean)

        for send in last:
            send.wait_recv()
        for n in range(S):
            for part in range(3):
                place = part * S * lanes + n * lanes
                attn_ref[:, place : place + lanes] = w_rows[n][:, part * lanes : (part + 1) * lanes].astype(F32)
        normed_sum.drain()
        for send in pending + swaps + small + last:
            send.wait_send()

    layer_out, tokens_grad, attn_grad, output_grad, gate_grad, up_grad, down_grad, sums = pl.pallas_call(
        kernel_h,
        in_specs=[ANY] * 2 + [VMEM] * 17,
        out_specs=[VMEM] * 8,
        out_shape=[
            shape((rows, width)),
            shape((rows, width), F32),
            shape((cut, 3 * S * lanes), F32),
            shape((cut, width), F32),
            shape((cut, S * hidden), F32),
            shape((cut, S * hidden), F32),
            shape((down_rows, width), F32),
            shape((8, 128), F32),
        ],
        scratch_shapes=[
            pltpu.VMEM((own_heads, dim, group), BF16),
            pltpu.VMEM((F, 2 * dim, group), BF16),
            pltpu.VMEM((S, cut, hidden), BF16),
            pltpu.VMEM((S, cut, hidden), BF16),
            pltpu.VMEM((S, cut, width), BF16),
            pltpu.VMEM((S, cut, hidden), BF16),
            pltpu.VMEM((S, cut, hidden), BF16),
            pltpu.VMEM((S, cut, width), BF16),
            pltpu.VMEM((down_rows, width), BF16),
            pltpu.VMEM((down_rows, width), BF16),
            dma,
            dma,
            pltpu.VMEM((group, 3 * lanes), BF16),
            pltpu.VMEM((S, rows, width), BF16),
            pltpu.VMEM((S, rows, width), BF16),
            pltpu.VMEM((S, rows, width), BF16),
            pltpu.VMEM((S, F, cut, 3 * lanes), BF16),
            pltpu.VMEM((F, S, cut, 3 * lanes), BF16),
            pltpu.VMEM((S, cut, 3 * lanes), BF16),
            pltpu.VMEM((S, cut, 3 * lanes), BF16),
            pltpu.VMEM((chunks, 8, 128), F32),
            pltpu.VMEM((count, 8, 128), F32),
            *[dma((groups,))] * 2,
            *[dma((F,))] * 2,
            dma((2,)),
            *[dma((3, S))] * 2,
            *[dma((2, S))] * 2,
            *[dma((F,))] * 2,
            *[dma((S,))] * 2,
            *[dma((count,))] * 2,
        ],
        compiler_params=pltpu.CompilerParams(
            collective_id=4, has_side_effects=True, vmem_limit_bytes=VMEM_BYTES
        ),
    )(
        query_grad, kv_grad, gate_got, up_got, output_got, down_got, out_terms, own_middle, middle_grad, raw, cosine, sine,
        gain_query[:, None], gain_key[:, None], gain_attn[None, :], w_qkv, x_parts, feed_gain, bias_row,
    )
    place = lax.rem((s * F + f) * cut, 128)
    return (
        layer_out,
        tokens_grad,
        attn_grad,
        output_grad,
        gate_grad,
        up_grad,
        down_grad,
        lax.dynamic_slice_in_dim(sums[0], place, cut),
        lax.dynamic_slice_in_dim(sums[1], place, cut),
        sums[2, :dim],
        sums[2, dim : 2 * dim],
        sums[3, : 2 * heads].reshape(heads, 2),
    )


def solution(mesh):
    by_token, by_fsdp, by_owner = P(("fsdp", "seq"), None), P("fsdp", None), P(("seq", "fsdp"), None)
    in_specs = (
        by_token,
        by_token,
        P(),
        P(),
        P(),
        P(),
        by_fsdp,
        P(),
        P(),
        P(),
        by_fsdp,
        P(),
        by_fsdp,
        by_fsdp,
        by_fsdp,
    )
    out_specs = (
        (by_token, by_token) + (by_owner,) * 5 + (P(("seq", "fsdp")),) * 2 + (P(),) * 3
    )
    return jax.shard_map(
        per_device, mesh=mesh, in_specs=in_specs, out_specs=out_specs, check_vma=False
    )
```

profile of v0, /device:TPU:0, one launch (start us, length us, event | category | flops | bytes accessed | tf_op | source)
XLA Modules:
  0.0 256.2 jit_solution(3240144608949814519)
XLA Ops:
  0.7 0.7 reshape_reshape.3
  1.4 0.6 dynamic-slice_bitcast_fusion.ids_mine_ref
  2.0 1.3 dynamic_slice.17
  3.3 1.4 copy.33.gain_q_ref
  4.7 1.4 copy.34.gain_k_ref
  6.1 0.6 multiply_power_fusion.freq_ref
  6.7 1.4 copy.35.bias_ref
  8.0 53.6 %shard_map.238 = (bf16[4,128,1024]{2,1,0:T(8,128)(2,1)}, bf16[1024,768]{1,0:T(8,128)(2,1)}, f32[2,4,64,512]{3,2,1,0:T(8,128)}, bf16[4,128,1024]{2,1,0:T(8,128)(2...) custom-call(bf16[128,1024]{1,0:T(8,128)(2,1)} %x_ref.1, ...), custom_call_target="tpu_custom_call" | custom-call | flops 1000000000 | bytes 100000000 | tf_op jit(solution)/shard_map/pallas_call | solution.py:600
  61.6 44.7 %shard_map.239 = (f32[4,64,512]{2,1,0:T(8,128)}, f32[4,1,512]{2,1,0:T(1,128)}, bf16[16,64,512]{2,1,0:T(8,128)(2,1)}, bf16[1024,1024]{1,0:T(8,128)(2,1)}, bf16[10...) custom-call(bf16[4,4,64,128]{3,2,1,0:T(8,128)(2,1)} %get-tuple-element.52.q_ref.refs_0_, ...), custom_call_target="tpu_custom_call" | custom-call | flops 20000000000 | bytes 100000000 | tf_op jit(solution)/shard_map/pallas_call | solution.py:763
  106.3 47.3 %shard_map.240 = (bf16[4,4,64,128]{3,2,1,0:T(8,128)(2,1)}, f32[128,1024]{1,0:T(8,128)}, f32[128,1024]{1,0:T(8,128)}, f32[1,1024]{1,0:T(1,128)}, bf16[4,128,1024]...) custom-call(bf16[1024,512]{1,0:T(8,128)(2,1)} %bitcast.32, ...), custom_call_target="tpu_custom_call" | custom-call | flops 10000000000 | bytes 100000000 | tf_op jit(solution)/shard_map/pallas_call | solution.py:955
  153.6 30.8 %shard_map.241 = (bf16[4,64,512]{2,1,0:T(8,128)(2,1)}, bf16[8,128,512]{2,1,0:T(8,128)(2,1)}, f32[2,8,256]{2,1,0:T(8,128)}, bf16[4,4,32,1024]{3,2,1,0:T(8,128)(2,...) custom-call(bf16[4,4,64,128]{3,2,1,0:T(8,128)(2,1)} %get-tuple-element.52.q_ref.refs_0_, ...), custom_call_target="tpu_custom_call" | custom-call | tf_op jit(solution)/shard_map/pallas_call | solution.py:1032
  184.5 0.8 reduce_sum.9
  185.3 0.6 fusion.3
  187.2 0.7 maximum_bitcast_fusion
  187.9 0.1 reshape.61
  188.0 0.5 pad.4.bias_ref
  188.5 55.0 %shard_map.242 = (bf16[128,1024]{1,0:T(8,128)(2,1)}, f32[128,1024]{1,0:T(8,128)}, f32[32,3072]{1,0:T(8,128)}, f32[32,1024]{1,0:T(8,128)}, f32[32,4096]{1,0:T(8,1...) custom-call(bf16[4,64,512]{2,1,0:T(8,128)(2,1)} %get-tuple-element.69.dq_ref, ...), custom_call_target="tpu_custom_call" | custom-call | tf_op jit(solution)/shard_map/pallas_call | solution.py:1260
  243.6 0.0 copy-start.3
  243.6 0.0 copy-start.2
  243.6 0.8 fusion.2
  244.4 0.6 fusion
  245.0 0.7 slice_reduce_fusion
  245.7 0.1 reshape_squeeze.3
  245.7 0.6 copy.38
  246.4 1.3 slice_bitcast_fusion
  247.7 1.7 copy.47
  249.4 1.9 copy.48
  251.3 1.8 copy.49
  253.1 0.7 copy.50
  253.8 0.8 copy.51
  254.6 0.8 copy.52
  255.4 0.8 copy.53
  (8 shorter events, 0.0 us)
Async XLA Ops:
  243.6 9.5 %copy-start.3 = (f32[32,1024]{1,0:T(8,128)S(1)}, f32[32,1024]{1,0:T(8,128)}, u32[]{:S(2)}) copy-start(f32[32,1024]{1,0:T(8,128)} %get-tuple-element.139) | copy-start | bytes 393220
  243.6 10.2 %copy-start.2 = (f32[32,4096]{1,0:T(8,128)S(1)}, f32[32,4096]{1,0:T(8,128)}, u32[]{:S(2)}) copy-start(f32[32,4096]{1,0:T(8,128)} %get-tuple-element.140) | copy-start | bytes 1572868
  243.6 11.0 %copy-start.1 = (f32[32,4096]{1,0:T(8,128)S(1)}, f32[32,4096]{1,0:T(8,128)}, u32[]{:S(2)}) copy-start(f32[32,4096]{1,0:T(8,128)} %get-tuple-element.141) | copy-start | bytes 1572868
  249.4 6.0 %copy-start = (f32[128,1024]{1,0:T(8,128)S(1)}, f32[128,1024]{1,0:T(8,128)}, u32[]{:S(2)}) copy-start(f32[128,1024]{1,0:T(8,128)} %get-tuple-element.142) | copy-start | bytes 1572868
where the time goes:
time: 257 us; the launch traced here: 256 us
  Pallas kernels  231 us (90%)
  local copies, waits for them, and re-layouts  20.5 us (8%)
    pallas_call x1, Pallas kernels, per_device(): pl.pallas_call(kernel_h, in_specs=[ANY] * 2 + [VMEM] * 17, out_specs=[VME...  55 us
    pallas_call x1, Pallas kernels, per_device(): pl.pallas_call(kernel_a, in_specs=[VMEM, ANY, ANY] + [VMEM] * 8 + [smem]...  53.6 us
    pallas_call x1, Pallas kernels, per_device(): pl.pallas_call(kernel_c, in_specs=[ANY] * 7 + [VMEM], out_specs=[ANY] + [...  47.3 us
    pallas_call x1, Pallas kernels, per_device(): pl.pallas_call(kernel_b, in_specs=[VMEM] * 4 + [ANY] * 3, out_specs=[VMEM...  44.7 us
    pallas_call x1, Pallas kernels, per_device(): pl.pallas_call(kernel_g, in_specs=[VMEM] * 7 + [ANY] * 3, out_specs=[VMEM...  30.8 us
    unnamed x17, local copies, waits for them, and re-layouts  10.4 us

commit v1 on v0

v1 whole, which is shorter than its diff:
```python
import functools

import jax
import jax.numpy as jnp
from jax import lax
from jax.experimental import pallas as pl
from jax.experimental.pallas import tpu as pltpu
from jax.sharding import PartitionSpec as P

EPSILON = 1e-06
F32, BF16 = jnp.float32, jnp.bfloat16
VARIATES = 8
AWAY = 1024.0
QUERY_BLOCK = 256
LSE_ROW, VAR_ROW = 32, 40
MESH = pl.DeviceIdType.MESH
ANY = pl.BlockSpec(memory_space=pl.ANY)
VMEM = pl.BlockSpec(memory_space=pltpu.VMEM)
VMEM_BYTES = 60 * 2**20


def nn(a, b):
    return jnp.dot(a, b, preferred_element_type=F32)


def nt(a, b):
    return lax.dot_general(a, b, (((1,), (1,)), ((), ())), preferred_element_type=F32)


def tn(a, b):
    return lax.dot_general(a, b, (((0,), (0,)), ((), ())), preferred_element_type=F32)


def pieces(values):
    high = values.astype(BF16).astype(F32)
    middle = (values - high).astype(BF16).astype(F32)
    return high, middle, (values - high - middle).astype(BF16).astype(F32)


def send_all(plan, send_sems, recv_sems, local_sems):
    remote, local = plan
    copies = []
    for n, (src, dst, device, may_send, may_receive) in enumerate(remote):
        copy = pltpu.make_async_remote_copy(
            src_ref=src,
            dst_ref=dst,
            send_sem=send_sems.at[n],
            recv_sem=recv_sems.at[n],
            device_id=device,
            device_id_type=MESH,
        )
        when(may_send, copy.start)
        copies.append((copy, may_send, may_receive))
    locals_ = []
    for n, (src, dst, may) in enumerate(local):
        copy = pltpu.make_async_copy(src, dst, local_sems.at[n])
        when(may, copy.start)
        locals_.append((copy, may))

    def finish():
        for copy, may in locals_:
            when(may, copy.wait)
        for copy, may_send, may_receive in copies:
            when(may_send, copy.wait_send)
            when(may_receive, copy.wait_recv)

    return finish


def when(condition, action):
    if condition is None:
        action()
    else:
        pl.when(condition)(action)


def greet(devices):
    barrier = pltpu.get_barrier_semaphore()
    for device in devices:
        pl.semaphore_signal(barrier, inc=1, device_id=device, device_id_type=MESH)
    pl.semaphore_wait(barrier, len(devices))


class Line:
    def __init__(self, block, sems, s, f, S):
        self.block, (self.sent, self.got) = block, sems
        self.s, self.f, self.S = s, f, S

    def hop(self, plane, slot, step):
        ref = self.block(plane, slot)
        return pltpu.make_async_remote_copy(
            src_ref=ref,
            dst_ref=ref,
            send_sem=self.sent.at[plane, slot, int(step > 0)],
            recv_sem=self.got.at[plane, slot],
            device_id=(self.s + step, self.f),
            device_id_type=MESH,
        )

    def each_hop(self, slot, distance, action):
        s, S = self.s, self.S
        pl.when((s - distance + 1) * (S - 1 - s) > 0)(
            lambda: action(self.hop(s - distance, slot, 1))
        )
        pl.when((S - s - distance) * s > 0)(lambda: action(self.hop(s + distance, slot, -1)))

    def send(self, slot):
        self.each_hop(slot, 0, lambda hop: hop.start())

    def arrive(self, slot, distance):
        s, S = self.s, self.S
        pl.when(s - distance >= 0)(lambda: self.hop(s - distance, slot, 1).wait_recv())
        pl.when(s + distance < S)(lambda: self.hop(s + distance, slot, -1).wait_recv())
        self.each_hop(slot, distance, lambda hop: hop.start())

    def drain(self, slot):
        for distance in range(self.S):
            self.each_hop(slot, distance, lambda hop: hop.wait_send())


def line_sems(S, slots):
    return [pltpu.SemaphoreType.DMA((S, slots, 2)), pltpu.SemaphoreType.DMA((S, slots))]


class LineSum:
    def __init__(self, terms, from_left, from_right, sems, s, f, S):
        self.terms, self.from_left, self.from_right = terms, from_left, from_right
        self.sent, self.got = sems
        self.s, self.f, self.S = s, f, S

    def hop(self, t, to_right):
        return pltpu.make_async_remote_copy(
            src_ref=self.terms.at[t],
            dst_ref=(self.from_left if to_right else self.from_right).at[t],
            send_sem=self.sent.at[int(to_right), t],
            recv_sem=self.got.at[int(to_right), t],
            device_id=(self.s + (1 if to_right else -1), self.f),
            device_id_type=MESH,
        )

    def take(self, t, to_right):
        self.hop(t, to_right).wait_recv()
        came = (self.from_left if to_right else self.from_right)[t]
        self.terms[t] = (self.terms[t].astype(F32) + came.astype(F32)).astype(BF16)

    def step(self, time, now=True):
        s, S = self.s, self.S
        n = time - s
        here = (n >= 0) & (S - 1 - n >= s) & now
        pl.when(here & (s >= 1))(lambda: self.take(S - 1 - n, True))
        pl.when(here & (S - 1 - n > s))(lambda: self.hop(S - 1 - n, True).start())
        m = time - (S - 1 - s)
        here = (m >= 0) & (m <= s) & now
        pl.when(here & (s < S - 1))(lambda: self.take(m, False))
        pl.when(here & (m < s))(lambda: self.hop(m, False).start())

    def drain(self):
        for t in range(self.S):
            pl.when(self.s < t)(lambda t=t: self.hop(t, True).wait_send())
            pl.when(self.s > t)(lambda t=t: self.hop(t, False).wait_send())


def flipped(f, bit):
    step = 2**bit
    return f + step - 2 * step * lax.rem(f // step, 2)


class CubeGather:
    def __init__(self, block, own, sems, s, f, F):
        self.block, self.own, (self.sent, self.shared, self.got) = block, own, sems
        self.s, self.f, self.F = s, f, F
        bits = list(range(1, F.bit_length() - 1))
        self.orders = (bits, bits[::-1])

    def copy(self, g, half, sem, to, own=False):
        ref = self.block(g, half)
        return pltpu.make_async_remote_copy(
            src_ref=self.own(half) if own else ref,
            dst_ref=ref,
            send_sem=sem,
            recv_sem=self.got.at[g, half],
            device_id=(self.s, to),
            device_id_type=MESH,
        )

    def held(self, half, rounds):
        masks = [((), 0)]
        for n, bit in enumerate(self.orders[half][:rounds]):
            masks += [(mask + (bit,), n + 1) for mask, _ in list(masks)]
        return masks

    def device(self, mask):
        g = self.f
        for bit in mask:
            g = flipped(g, bit)
        return g

    def sends(self, half, since):
        rounds = len(self.orders[half])
        out = []
        for place, (mask, came) in enumerate(self.held(half, rounds)):
            for n in range(came, rounds):
                if came == since:
                    out.append((n, place, mask))
        return out

    def send(self, half, n, place, mask):
        bit = self.orders[half][n]
        sem = self.sent.at[half, n, place]
        return self.copy(self.device(mask), half, sem, flipped(self.f, bit), not mask)

    def shares(self, half, since):
        return [
            self.copy(
                self.device(mask), half, self.shared.at[half, place], flipped(self.f, 0), not mask
            )
            for place, (mask, came) in enumerate(self.held(half, len(self.orders[half])))
            if came == since
        ]

    @property
    def rounds(self):
        return len(self.orders[0])

    def start(self):
        for half in range(2):
            self.send(half, 0, 0, ()).start()
        for half in range(2):
            self.shares(half, 0)[0].start()

    def step(self, number):
        for half in range(2):
            shares = self.shares(half, number)
            for share in shares:
                share.wait_recv()
            if number < self.rounds:
                for which in self.sends(half, number) + self.sends(half, 0)[number : number + 1]:
                    if which[0] == number or which[1]:
                        self.send(half, *which).start()
            for share in shares:
                share.start()

    def finish(self):
        for half in range(2):
            for place, (mask, _) in enumerate(self.held(half, self.rounds)):
                g = flipped(self.device(mask), 0)
                self.copy(g, half, self.shared.at[half, place], self.f).wait_recv()

    def drain(self):
        for half in range(2):
            for number in range(self.rounds + 1):
                for which in self.sends(half, number):
                    self.send(half, *which).wait_send()
                for share in self.shares(half, number):
                    share.wait_send()


def cube_sems(F):
    rounds = F.bit_length() - 2
    return [
        pltpu.SemaphoreType.DMA((2, rounds, F // 4)),
        pltpu.SemaphoreType.DMA((2, F // 2)),
        pltpu.SemaphoreType.DMA((F, 2)),
    ]


def shape(dims, dtype=BF16):
    return jax.ShapeDtypeStruct(tuple(dims), dtype)


def join(a, b):
    return jnp.concatenate([a, b], axis=0)


def side_by_side(ref, *index):
    return jnp.concatenate([ref[(*index, n)] for n in range(ref.shape[len(index)])], axis=1)


def forward_group(j, q_ref, kv_ref, qa_ref, ka_ref, att_ref, lse_ref, o_ref):
    width, rows = att_ref.shape[1:]
    span = q_ref.shape[-1]
    sub = QUERY_BLOCK // span

    def block(i, _):
        cols = pl.ds(pl.multiple_of(i * QUERY_BLOCK, QUERY_BLOCK), QUERY_BLOCK)
        q_t = jnp.concatenate([q_ref[j, i * sub + n] for n in range(sub)], axis=1)
        queries = join(q_t, qa_ref[j, :, cols]).T
        total = jnp.zeros((QUERY_BLOCK, 2 * width), F32)
        for g in range(kv_ref.shape[0]):
            kv = side_by_side(kv_ref, g)
            keys = join(kv[:width], ka_ref[g])
            values = join(kv[width:], jnp.ones((width, rows), BF16))
            weights = jnp.exp(nn(queries, keys)).astype(BF16)
            total += nt(weights, values)
        total = total.T
        weight_sum = total[width : width + 1]
        attended = total[:width] / weight_sum
        att_ref[j, :, cols] = attended
        o_ref[j, :, cols] = attended.astype(BF16)
        lse_ref[j, :, cols] = jnp.log(weight_sum)
        return 0

    lax.fori_loop(0, rows // QUERY_BLOCK, block, 0)


def with_rows(base, first, rows):
    index = lax.broadcasted_iota(jnp.int32, base.shape, 0)
    for n, row in enumerate(rows):
        base = jnp.where(index == first + n, row, base)
    return base


def rms_scale(vector, gain, axis=-1):
    return vector * lax.rsqrt(jnp.mean(vector * vector, axis=axis, keepdims=True) + EPSILON) * gain


def per_device(
    tokens,
    cotangent,
    doc_starts,
    variate_ids,
    time_ids,
    gain_attn,
    w_attn,
    gain_query,
    gain_key,
    variate_bias,
    w_output,
    gain_feed,
    w_gate,
    w_up,
    w_down,
):
    S, F = lax.axis_size("seq"), lax.axis_size("fsdp")
    s, f = lax.axis_index("seq"), lax.axis_index("fsdp")
    rows, width = tokens.shape
    heads = variate_bias.shape[0]
    dim = gain_query.shape[0]
    own_heads = heads // S
    splits = F // own_heads
    group = rows * S
    groups = F // splits
    hidden = w_down.shape[0] * F // S
    half = F // 2
    cut = width // (S * F)
    lanes = own_heads * dim

    def along_seq(s, f):
        return [(lax.rem(s + d, S), f) for d in range(1, S)]

    def along_fsdp(s, f):
        return [(s, lax.rem(f + d, F)) for d in range(1, F)]

    def along_both(s, f):
        return along_seq(s, f) + along_fsdp(s, f)

    def like_parts(s, f):
        return [
            (lax.rem(s + a, S), lax.rem(f + b * splits, F))
            for a in range(S)
            for b in range(groups)
            if a or b
        ]

    def everyone(s, f):
        return [(lax.rem(s + a, S), lax.rem(f + b, F)) for a in range(S) for b in range(F) if a or b]

    def seq_swap(s, f, src, dst):
        remote = [(src.at[t[0]], dst.at[s], t, None, None) for t in along_seq(s, f)]
        return remote, [(src.at[s], dst.at[s], None)]

    per_plane = F // S
    down_rows = w_down.shape[0] // S
    local_rows = w_attn.shape[0]
    whole_tiles = down_rows % 128 == 0

    def unit_place(s, f):
        return lax.rem(f, per_plane) * S + lax.rem(f // per_plane + s, S)

    def unit_block(s, g):
        holder = lax.rem(lax.rem(g, S) - s + S, S) * per_plane + g // S
        return holder * S + lax.rem(g, S)

    def units(w):
        if whole_tiles:
            return w
        blocks = w.reshape(w.shape[0], S * F, down_rows)
        return jnp.concatenate(
            [lax.dynamic_index_in_dim(blocks, unit_block(s, g), 1, False) for g in range(F)], axis=1
        )

    def pair(s, f):
        return (s, flipped(f, 0))

    def same_parity(s, f):
        return [(s, lax.rem(f + 2 * d, F)) for d in range(1, half)]

    def peers_a(s, f):
        return like_parts(s, f) + [(s, lax.rem(f + d, F)) for d in range(1, F) if d % splits]

    block = 256 if width % 256 == 0 and hidden % 256 == 0 else 128

    frequency = (10000.0 ** (-2.0 * jnp.arange(dim // 2, dtype=F32) / dim))[:, None]
    total = F * group

    def kernel_a(
        x_ref, cot_ref, w_ref, wo_ref, wd_ref, wg_ref, wu_ref, times_ref, ids_ref, freq_ref, gain_ref, gain_q_ref, gain_k_ref,
        gain_feed_ref, bias_ref, starts_ref,
        xs_out, ws_out, raw_out, cos_ref, sin_ref, ka_out, qa_out, qs_out, kvs_out, att_out, lse_ref,
        grads_ref, middle_ref, mid_grad_ref, feed_ref, out_ref, gate_got, up_got, down_half, output_half,
        xs_ref, ws_ref, raw_ref, cots_ref, ka_ref, qa_ref, q_ref, kv_ref, att_ref, heads_ref, wos_ref, gates_ref, ups_ref,
        downs_ref, mid_v, n_v, n_t, hid_v, hid_t, gl_v, ul_v, u_ref, from_left, from_right,
        gate_part, up_part, down_part, output_part, gate_other, up_other, down_other, output_other, gate_half, up_half,
        hg_ref, u_sent, u_got, pair_sent, pair_got, spread_sent, spread_got, own_sem, f_sent, f_got, out_sem,
        q_out, kv_out, o_ref, gate_own, up_own,
        w_sem, unit_sem, here_sem, x_sent, x_got, c_sent, c_got, kv_sent, kv_shared, kv_got, q_sent, q_got,
        o_sent, h_sent, h_got, *cube_refs,
    ):
        s, f = lax.axis_index("seq"), lax.axis_index("fsdp")
        column, part = f // splits, lax.rem(f, splits)
        loads = []
        for n in range(3):
            src = w_ref.at[:, pl.ds(pl.multiple_of(n * S * lanes + s * lanes, 128), lanes)]
            dst = ws_ref.at[pl.ds(f * local_rows, local_rows), pl.ds(n * lanes, lanes)]
            loads.append(pltpu.make_async_copy(src, dst, w_sem.at[n]))
        unit_loads = []
        for n, (src, dst) in enumerate(((wg_ref, gate_own), (wu_ref, up_own))):
            for g in range(F if whole_tiles else 1):
                if whole_tiles:
                    cols = pl.ds(pl.multiple_of(unit_block(s, g) * down_rows, 128), down_rows)
                    src_, dst_ = src.at[:, cols], dst.at[:, pl.ds(g * down_rows, down_rows)]
                else:
                    src_, dst_ = src, dst
                unit_loads.append(pltpu.make_async_copy(src_, dst_, unit_sem.at[n, g]))
        for load in loads + unit_loads:
            load.start()
        xs_ref[s] = x_ref[...]
        cots_ref[s] = cot_ref[...]
        greet(peers_a(s, f))
        xs = Line(lambda plane, slot: xs_ref.at[plane], (x_sent, x_got), s, f, S)
        cots = Line(lambda plane, slot: cots_ref.at[plane], (c_sent, c_got), s, f, S)
        xs.send(0)

        def rows_of(ref, size, place=lambda g: g):
            return lambda g, half: ref.at[pl.ds(place(g) * size + half * (size // 2), size // 2)]

        def half_of(ref, size):
            return lambda half: ref.at[pl.ds(half * (size // 2), size // 2)]

        down_own = wd_ref.at[lax.rem(f // per_plane + s, S)]
        down_place = unit_place(s, f)
        blocks = (
            (rows_of(ws_ref, local_rows), lambda half: rows_of(ws_ref, local_rows)(f, half)),
            (rows_of(wos_ref, local_rows), half_of(wo_ref, local_rows)),
            (rows_of(gates_ref, local_rows), half_of(gate_own, local_rows)),
            (rows_of(ups_ref, local_rows), half_of(up_own, local_rows)),
            (rows_of(downs_ref, down_rows, lambda g: unit_place(s, g)), half_of(down_own, down_rows)),
        )
        ws, wos, gates, ups, downs = [
            CubeGather(block, own, cube_refs[3 * n : 3 * n + 3], s, f, F) for n, (block, own) in enumerate(blocks)
        ]
        for load in loads:
            load.wait()
        ws.start()
        for load in unit_loads:
            load.wait()
        mine = pl.ds(f * local_rows, local_rows)
        here = [
            pltpu.make_async_copy(wo_ref, wos_ref.at[mine], here_sem.at[0]),
            pltpu.make_async_copy(gate_own, gates_ref.at[mine], here_sem.at[1]),
            pltpu.make_async_copy(up_own, ups_ref.at[mine], here_sem.at[2]),
            pltpu.make_async_copy(down_own, downs_ref.at[pl.ds(down_place * down_rows, down_rows)], here_sem.at[3]),
        ]
        for copy in here:
            copy.start()

        own_cols = pl.ds(pl.multiple_of(f * group, 128), group)
        angles = freq_ref[...] * times_ref[:, own_cols].astype(F32)
        cos_ref[...] = jnp.cos(angles)
        sin_ref[...] = jnp.sin(angles)
        mine_only = lax.broadcasted_iota(jnp.int32, (2, heads), 1) == s * own_heads + column
        biases = jnp.sum(jnp.where(mine_only, bias_ref[...], 0.0), axis=1, keepdims=True)
        difference = pieces(jnp.broadcast_to(biases[0:1] - biases[1:2], (VARIATES, group)))
        index = lax.broadcasted_iota(jnp.int32, (VARIATES, group), 0)

        def marks(g):
            ids = ids_ref[:, pl.ds(pl.multiple_of(g * group, 128), group)]
            positions = g * group + lax.broadcasted_iota(jnp.int32, (VARIATES, group), 1)
            docs = jnp.zeros((VARIATES, group), jnp.int32) - 1
            for n in range(doc_starts.shape[0]):
                docs = docs + (starts_ref[n] <= positions).astype(jnp.int32)
            return (docs == index).astype(F32), (ids == index).astype(F32)

        for g in range(F):
            doc, var = marks(g)
            tail = (index < 3).astype(F32)
            none = jnp.zeros((dim - LSE_ROW - VARIATES, group), F32)
            ka_ref[g] = jnp.concatenate([var, var, var, 1.0 - doc, tail, none]).astype(BF16)
        for j in range(groups):
            doc, var = marks(j * splits + part)
            none = jnp.zeros((VARIATES, group), F32)
            rest = jnp.zeros((dim - VAR_ROW - VARIATES, group), F32)
            scaled = [var * piece for piece in difference]
            qa_ref[j] = jnp.concatenate([*scaled, doc * -AWAY, none, var, rest]).astype(BF16)
        gain_q, gain_k = [
            jnp.broadcast_to(ref[...], (128, dim)).T[:, :rows] for ref in (gain_q_ref, gain_k_ref)
        ]

        def kv_copy(g, b, src, sem, to):
            return pltpu.make_async_remote_copy(
                src_ref=src, dst_ref=kv_ref.at[g, b], send_sem=sem, recv_sem=kv_got.at[g, b],
                device_id=(s, to), device_id_type=MESH,
            )

        def to_heads(b, d):
            to = lax.rem(f + 2 * d, F)
            return kv_copy(f, b, kv_out.at[b, to // splits], kv_sent.at[b, d], to)

        def to_neighbour(b, d):
            g = lax.rem(f + 2 * d, F)
            src = kv_ref.at[g, b] if d else kv_out.at[b, column]
            return kv_copy(g, b, src, kv_shared.at[b, d], flipped(f, 0))

        def queries_to_heads(b, d):
            to = lax.rem(f + d * splits, F)
            return pltpu.make_async_remote_copy(
                src_ref=q_out.at[b, to // splits], dst_ref=q_ref.at[column, b], send_sem=q_sent.at[b, d],
                recv_sem=q_got.at[column, b], device_id=(s, to), device_id_type=MESH,
            )

        def project(b):
            normed = rms_scale(xs_ref[b].astype(F32), gain_ref[...]).astype(BF16)
            projected = nn(normed, ws_ref[...]).T.reshape(3, own_heads, dim, rows)
            cols = pl.ds(pl.multiple_of(b * rows, rows), rows)
            cosine, sine = cos_ref[:, cols], sin_ref[:, cols]

            def turned(raw, gain):
                raw = rms_scale(raw, gain, axis=1)
                front, back = raw[:, : dim // 2], raw[:, dim // 2 :]
                return jnp.concatenate(
                    [front * cosine - back * sine, front * sine + back * cosine], axis=1
                )

            raw_ref[0, :, :, cols] = projected[0]
            raw_ref[1, :, :, cols] = projected[1]
            q_out[b] = (turned(projected[0], gain_q).astype(BF16).astype(F32) * dim**-0.5).astype(BF16)
            kv_out[b, :, :dim] = turned(projected[1], gain_k).astype(BF16)
            kv_out[b, :, dim:] = projected[2].astype(BF16)
            for d in range(1, half):
                to_heads(b, d).start()
            for d in range(1, groups):
                queries_to_heads(b, d).start()
            to_neighbour(b, 0).start()
            kv_ref[f, b] = kv_out[b, column]
            q_ref[column, b] = q_out[b, column]

        def share(b):
            for d in range(1, half):
                to_neighbour(b, d).wait_recv()
                to_neighbour(b, d).start()

        for number in range(1, ws.rounds + 1):
            ws.step(number)
        wos.start()
        ws.finish()
        project(s)
        for distance in range(1, S):
            xs.arrive(0, distance)
            if distance == S - 1:
                cots.send(0)
            pl.when(s - distance >= 0)(lambda distance=distance: project(s - distance))
            pl.when(s + distance < S)(lambda distance=distance: project(s + distance))
            if distance == S - 2:
                wos.step(1)

        def share_all(b, _):
            share(b)
            return 0

        lax.fori_loop(0, S, share_all, 0)
        gates.start()

        def last(b, _):
            for d in range(half):
                g = lax.rem(flipped(f, 0) + 2 * d, F)
                kv_copy(g, b, kv_ref.at[g, b], kv_shared.at[b, d], f).wait_recv()
            for d in range(1, groups):
                g = lax.rem(f + d * splits, F)
                pltpu.make_async_remote_copy(
                    src_ref=q_out.at[b, 0], dst_ref=q_ref.at[g // splits, b], send_sem=q_sent.at[b, d],
                    recv_sem=q_got.at[g // splits, b], device_id=(s, g), device_id_type=MESH,
                ).wait_recv()
            return 0

        lax.fori_loop(0, S, last, 0)
        ups.start()
        downs.start()

        own = s * own_heads + column

        def to_column(turn):
            j = lax.rem(column + turn, groups)
            return pltpu.make_async_remote_copy(
                src_ref=o_ref.at[j], dst_ref=heads_ref.at[own], send_sem=o_sent.at[turn], recv_sem=h_got.at[turn, 0],
                device_id=(s, j * splits + part), device_id_type=MESH,
            )

        def along(turn, d):
            ref = heads_ref.at[s * own_heads + lax.rem(column - turn + groups, groups)]
            return pltpu.make_async_remote_copy(
                src_ref=ref, dst_ref=ref, send_sem=h_sent.at[turn, d], recv_sem=h_got.at[turn, d],
                device_id=(lax.rem(s + d, S), f), device_id_type=MESH,
            )

        for turn in range(groups + 1):
            if turn < groups:
                j = lax.rem(column + turn, groups)
                forward_group(j, q_ref, kv_ref, qa_ref, ka_ref, att_ref, lse_ref, o_ref)
                if turn:
                    to_column(turn).start()
                else:
                    heads_ref[own] = o_ref[j]
            if turn != 1:
                came = max(turn - 1, 0)
                if came:
                    to_column(came).wait_recv()
                for d in range(1, S):
                    along(came, d).start()
            if turn + 1 < S:
                cots.arrive(0, turn + 1)
            if turn == 0:
                gates.step(1)
            if turn == 2:
                for number in range(2, wos.rounds + 1):
                    wos.step(number)
                    gates.step(number)
            if turn == 3:
                ups.step(1)
                downs.step(1)
        for distance in range(groups + 2, S):
            cots.arrive(0, distance)
        for number in range(2, ups.rounds + 1):
            ups.step(number)
            downs.step(number)

        flushes = [
            pltpu.make_async_copy(src, dst, out_sem.at[n])
            for n, (src, dst) in enumerate(
                (
                    (xs_ref, xs_out), (ws_ref, ws_out), (raw_ref, raw_out), (ka_ref, ka_out), (qa_ref, qa_out),
                    (q_ref, qs_out), (kv_ref, kvs_out), (att_ref, att_out),
                )
            )
        ]
        for flush in flushes:
            flush.start()
        for turn in range(groups):
            for d in range(1, S):
                along(turn, d).wait_recv()
        for copy_ in here:
            copy_.wait()
        wos.finish()

        def copy(src, dst, sent, got, to):
            return pltpu.make_async_remote_copy(
                src_ref=src, dst_ref=dst, send_sem=sent, recv_sem=got, device_id=to, device_id_type=MESH
            )

        heads_rows = heads_ref[...].reshape(heads * dim, group).T
        for c in range(0, width, block):
            cs = slice(c, c + block)
            mid_v[:, cs] = xs_ref[:, :, cs].astype(F32).reshape(group, block) + nn(heads_rows, wos_ref[:, cs])
        normed = rms_scale(mid_v[...], gain_feed_ref[...]).astype(BF16)
        n_v[...] = normed
        n_t[...] = normed.T
        for gather in (gates, ups, downs):
            gather.finish()
        cot_rows = cots_ref[...].reshape(group, width)
        for c in range(0, hidden, block):
            cs = slice(c, c + block)
            gate_act, up_act = nn(n_v[...], gates_ref[:, cs]), nn(n_v[...], ups_ref[:, cs])
            hidden_grad = nt(cot_rows, downs_ref[cs, :])
            sigmoid = jax.nn.sigmoid(gate_act)
            silu = gate_act * sigmoid
            hidden_low = (silu * up_act).astype(BF16)
            hid_v[:, cs] = hidden_low
            hid_t[cs, :] = hidden_low.T
            gl_v[:, cs] = (hidden_grad * up_act * sigmoid * (1.0 + gate_act * (1.0 - sigmoid))).astype(BF16)
            ul_v[:, cs] = (hidden_grad * silu).astype(BF16)
        for c in range(0, width, block):
            cs = slice(c, c + block)
            grad = nt(gl_v[...], gates_ref[cs, :]) + nt(ul_v[...], ups_ref[cs, :])
            u_ref[:, :, cs] = grad.astype(BF16).reshape(S, rows, block)
        mid_sum = LineSum(u_ref, from_left, from_right, (u_sent, u_got), s, f, S)
        mid_sum.step(0)

        parity = lax.rem(f, 2)
        by_owner = (S, half, 2, cut, block)

        def exchange_halves(n, part, other):
            away = part.at[:, 1 - parity] if len(part.shape) == 4 else part.at[:, :, 1 - parity]
            send = copy(away, other, pair_sent.at[n], pair_got.at[n], pair(s, f))
            send.start()
            return send

        for c in range(0, hidden, block):
            cs = slice(c, c + block)
            gate_part[..., cs] = nn(n_t[...], gl_v[:, cs]).astype(BF16).reshape(by_owner)
        swaps = [exchange_halves(0, gate_part, gate_other)]
        for c in range(0, hidden, block):
            cs = slice(c, c + block)
            up_part[..., cs] = nn(n_t[...], ul_v[:, cs]).astype(BF16).reshape(by_owner)
        swaps.append(exchange_halves(1, up_part, up_other))
        for c in range(0, width, block):
            cs = slice(c, c + block)
            down_part[..., cs] = nn(hid_t[...], cots_ref[:, :, cs].reshape(group, block)).astype(BF16).reshape(half, 2, down_rows, block)
        swaps.append(exchange_halves(2, down_part, down_other))
        for c in range(0, width, block):
            cs = slice(c, c + block)
            out_ref[:, :, cs] = nn(hid_v[...], downs_ref[:, cs]).astype(BF16).reshape(S, rows, block)

        def spread(n, halves, got):
            here = pltpu.make_async_copy(halves.at[:, f // 2], got.at[f // 2], own_sem.at[n])
            here.start()
            sends = []
            for d, to in enumerate(same_parity(s, f)):
                send = copy(halves.at[:, to[1] // 2], got.at[f // 2], spread_sent.at[n, d], spread_got.at[n, d], to)
                send.start()
                sends.append(send)
            return here, sends

        def add(a, b):
            return (a.astype(F32) + b.astype(F32)).astype(BF16)

        swaps[0].wait_recv()
        gate_half[...] = add(gate_part[:, :, parity], gate_other[...])
        spreads = [spread(0, gate_half, gate_got)]
        mid_sum.step(1)
        swaps[1].wait_recv()
        up_half[...] = add(up_part[:, :, parity], up_other[...])
        spreads.append(spread(1, up_half, up_got))
        swaps[2].wait_recv()
        down_half[...] = add(down_part[:, parity], down_other[...])
        for time in range(2, S):
            mid_sum.step(time)

        middle = mid_v[pl.ds(pl.multiple_of(s * rows, rows), rows), :]
        grad = u_ref[s].astype(F32)
        inverse = lax.rsqrt(jnp.mean(middle * middle, axis=1, keepdims=True) + EPSILON)
        scaled = grad * gain_feed_ref[...]
        mean = jnp.mean(scaled * middle, axis=1, keepdims=True)
        own_cot = cots_ref[s].astype(F32)
        middle_grad = own_cot + inverse * scaled - middle * (inverse**3 * mean)
        middle_low = middle_grad.astype(BF16)
        hg_ref[...] = nt(wos_ref[...], middle_low).astype(BF16).reshape(heads, dim, rows)

        place = grads_ref.at[f // splits, s]
        grads_here = pltpu.make_async_copy(hg_ref.at[s * own_heads + f // splits], place, own_sem.at[2])
        grads_here.start()
        sends = []
        for n, to in enumerate(like_parts(s, f)):
            send = copy(hg_ref.at[to[0] * own_heads + to[1] // splits], place, f_sent.at[n], f_got.at[n], to)
            send.start()
            sends.append(send)

        middle_ref[...] = middle
        mid_grad_ref[...] = middle_grad
        feed_ref[...] = jnp.sum(grad * middle * inverse, axis=0, keepdims=True)
        own_heads_t = heads_ref[:, :, pl.ds(pl.multiple_of(s * rows, rows), rows)].reshape(heads * dim, rows)
        for c in range(0, width, block):
            cs = slice(c, c + block)
            output_part[..., cs] = nn(own_heads_t, middle_low[:, cs]).astype(BF16).reshape(by_owner)
        swaps.append(exchange_halves(3, output_part, output_other))
        swaps[3].wait_recv()
        output_half[...] = add(output_part[:, :, parity], output_other[...])
        grads_here.wait()
        for send in sends:
            send.wait()
        for here, others in spreads:
            here.wait()
            for send in others:
                send.wait()
        for swap in swaps:
            swap.wait_send()
        mid_sum.drain()

        for flush in flushes:
            flush.wait()
        def sent(b, _):
            for d in range(half):
                if d:
                    to_heads(b, d).wait_send()
                to_neighbour(b, d).wait_send()
            for d in range(1, groups):
                queries_to_heads(b, d).wait_send()
            return 0

        lax.fori_loop(0, S, sent, 0)
        xs.drain(0)
        cots.drain(0)
        ws.drain()
        for turn in range(groups):
            if turn:
                to_column(turn).wait_send()
            for d in range(1, S):
                along(turn, d).wait_send()
        for gather in (wos, gates, ups, downs):
            gather.drain()

    dma = pltpu.SemaphoreType.DMA
    wide = (S, half, 2, cut, hidden)
    wide_half = (S, half, cut, hidden)
    kept = [
        shape((S, rows, width)),
        shape((width, 3 * lanes)),
        shape((2, own_heads, dim, group), F32),
        shape((F, dim, group)),
        shape((groups, dim, group)),
        shape((groups, S, dim, rows)),
        shape((F, S, 2 * dim, rows)),
        shape((groups, dim, group), F32),
    ]
    (
        x_parts, w_qkv, raw, cosine, sine, key_marks, query_marks, q_all, kv_all, attended, log_sum,
        grad_heads, own_middle, middle_grad, feed_gain, out_part, gate_got, up_got, down_half, output_half,
    ) = pl.pallas_call(
        kernel_a,
        in_specs=[VMEM] * 2 + [ANY] * 5 + [VMEM] * 8 + [pl.BlockSpec(memory_space=pltpu.SMEM)],
        out_specs=[ANY] * 3 + [VMEM] * 2 + [ANY] * 5 + [VMEM] + [ANY] + [VMEM] * 4 + [ANY] * 2 + [VMEM] * 2,
        out_shape=[
            *kept[:3],
            shape((dim // 2, group), F32),
            shape((dim // 2, group), F32),
            *kept[3:],
            shape((groups, 1, group), F32),
            shape((groups, S, dim, rows)),
            shape((rows, width), F32),
            shape((rows, width), F32),
            shape((1, width), F32),
            shape((S, rows, width)),
            shape((half, S, cut, hidden)),
            shape((half, S, cut, hidden)),
            shape((half, down_rows, width)),
            shape((S, half, cut, width)),
        ],
        scratch_shapes=[
            *[pltpu.VMEM(kept[n].shape, kept[n].dtype) for n in range(3)],
            pltpu.VMEM((S, rows, width), BF16),
            *[pltpu.VMEM(one.shape, one.dtype) for one in kept[3:]],
            pltpu.VMEM((heads, dim, group), BF16),
            pltpu.VMEM((heads * dim, width), BF16),
            pltpu.VMEM((width, hidden), BF16),
            pltpu.VMEM((width, hidden), BF16),
            pltpu.VMEM((hidden, width), BF16),
            pltpu.VMEM((group, width), F32),
            pltpu.VMEM((group, width), BF16),
            pltpu.VMEM((width, group), BF16),
            pltpu.VMEM((group, hidden), BF16),
            pltpu.VMEM((hidden, group), BF16),
            pltpu.VMEM((group, hidden), BF16),
            pltpu.VMEM((group, hidden), BF16),
            *[pltpu.VMEM((S, rows, width), BF16)] * 3,
            *[pltpu.VMEM(wide, BF16)] * 2,
            pltpu.VMEM((half, 2, down_rows, width), BF16),
            pltpu.VMEM((S, half, 2, cut, width), BF16),
            *[pltpu.VMEM(wide_half, BF16)] * 2,
            pltpu.VMEM((half, down_rows, width), BF16),
            pltpu.VMEM((S, half, cut, width), BF16),
            *[pltpu.VMEM(wide_half, BF16)] * 2,
            pltpu.VMEM((heads, dim, rows), BF16),
            *[dma((2, S))] * 2,
            *[dma((4,))] * 2,
            *[dma((2, half))] * 2,
            dma((3,)),
            *[dma((S * groups,))] * 2,
            dma((len(kept),)),
            pltpu.VMEM((S, own_heads, dim, rows), BF16),
            pltpu.VMEM((S, own_heads, 2 * dim, rows), BF16),
            pltpu.VMEM((groups, dim, group), BF16),
            pltpu.VMEM((local_rows, hidden), BF16),
            pltpu.VMEM((local_rows, hidden), BF16),
            dma((3,)),
            dma((2, F)),
            dma((4,)),
            *line_sems(S, 1),
            *line_sems(S, 1),
            dma((S, half)),
            dma((S, half)),
            dma((F, S)),
            dma((S, groups)),
            dma((groups, S)),
            dma((groups,)),
            dma((groups, S)),
            dma((groups, S)),
            *[sem for _ in range(5) for sem in cube_sems(F)],
        ],
        compiler_params=pltpu.CompilerParams(
            collective_id=0, has_side_effects=True, vmem_limit_bytes=VMEM_BYTES
        ),
        cost_estimate=pl.CostEstimate(flops=2 * 10**10, bytes_accessed=10**8, transcendentals=10**7),
    )(
        tokens,
        cotangent,
        w_attn,
        w_output,
        w_down.reshape(S, down_rows, width),
        units(w_gate),
        units(w_up),
        time_ids[None, :],
        variate_ids[None, :],
        frequency,
        gain_attn[None, :],
        gain_query[None, :],
        gain_key[None, :],
        gain_feed[None, :],
        variate_bias.T,
        doc_starts,
    )

    count = S * F
    chunks = width // 128
    blocks = group // QUERY_BLOCK
    span = QUERY_BLOCK // rows
    small_rows = 8

    def kernel_g(
        q_ref, kv_ref, qa_ref, ka_ref, do_ref, att_ref, lse_ref, cos_ref, sin_ref, gain_q_ref, gain_k_ref, feed_ref,
        gain_ref, out_half, down_half, out_hbm, gate_hbm, up_hbm, raw_hbm, ws_hbm, xs_hbm,
        u_own, w_rows, gate_rows, up_rows, out_rows, down_moved, layer_own, vec_got,
        out_got, down_got, gate_got, up_got,
        qq_ref, dd_ref, dq_sum, kv_sum, kv_send, kv_other, dq_send, dqs, dkvs, gate_sum, up_sum, out_sum, down_sum,
        layer_ref, layer_left, layer_right, raw_ref, ws_ref, xs_ref, pg_ref, u_ref, from_left, from_right, w_part, w_got,
        w_sum, vec, bias_ref,
        load_sem, own_sem, spread_sent, spread_got, layer_sent, layer_got, swap_sent, swap_got, pair_sent, pair_got,
        dkv_sent, dkv_got, dq_sent, dq_got, u_sent, u_got, w_sent, w_arrived, rows_sent, rows_got, vec_sent, vec_arrived,
        down_sent, down_arrived,
    ):
        s, f = lax.axis_index("seq"), lax.axis_index("fsdp")
        column, part, parity = f // splits, lax.rem(f, splits), lax.rem(f, 2)

        def copy(src, dst, sent, got, to):
            return pltpu.make_async_remote_copy(
                src_ref=src, dst_ref=dst, send_sem=sent, recv_sem=got, device_id=to, device_id_type=MESH
            )

        loads = [
            pltpu.make_async_copy(src, dst, load_sem.at[n])
            for n, (src, dst) in enumerate(
                (
                    (out_hbm, layer_ref), (gate_hbm, gate_got), (up_hbm, up_got), (raw_hbm, raw_ref), (ws_hbm, ws_ref),
                    (xs_hbm, xs_ref),
                )
            )
        ]
        for load in loads:
            load.start()
        greet(everyone(s, f))

        spreads = []
        for n, (src, got) in enumerate(((out_half, out_got), (down_half, down_got))):
            pick = (lambda ref, g: ref.at[:, g]) if n == 0 else (lambda ref, g: ref.at[g])
            here = pltpu.make_async_copy(pick(src, f // 2), got.at[f // 2], own_sem.at[n])
            here.start()
            sends = []
            for d, to in enumerate(same_parity(s, f)):
                sends.append(copy(pick(src, to[1] // 2), got.at[f // 2], spread_sent.at[n, d], spread_got.at[n, d], to))
                sends[-1].start()
            spreads.append((here, sends))
        layer = LineSum(layer_ref, layer_left, layer_right, (layer_sent, layer_got), s, f, S)
        loads[0].wait()
        layer.step(0)
        swaps = []

        def swap_rows(n, got, total, rows_ref):
            total[...] = jnp.sum(got[...].astype(F32), axis=0).astype(BF16)
            rows_ref[s] = total[s]
            for d in range(1, S):
                to = lax.rem(s + d, S)
                swaps.append(copy(total.at[to], rows_ref.at[s], swap_sent.at[n, d], swap_got.at[n, d], (to, f)))
                swaps[-1].start()

        def rows_at(i):
            return pl.ds(pl.multiple_of(i * QUERY_BLOCK, QUERY_BLOCK), QUERY_BLOCK)

        def tokens_of(ref, i):
            j, first = i // blocks, (i % blocks) * span
            return jnp.concatenate([ref[j, first + n] for n in range(span)], axis=1)

        def ready(i, _):
            j, cols = i // blocks, rows_at(i % blocks)
            marks = qa_ref[j, :, cols].astype(F32)
            extra = with_rows(marks, LSE_ROW, pieces(-lse_ref[j, :, cols])).astype(BF16)
            qq_ref[rows_at(i), :] = join(tokens_of(q_ref, i), extra).T
            grad_t = tokens_of(do_ref, i)
            delta = jnp.sum(grad_t.astype(F32) * att_ref[j, :, cols], axis=0, keepdims=True)
            extra = with_rows(jnp.zeros((dim, QUERY_BLOCK), F32), 0, pieces(-delta)).astype(BF16)
            dd_ref[rows_at(i), :] = join(grad_t, extra).T
            return 0

        lax.fori_loop(0, groups * blocks, ready, 0)
        for load in loads[1:3]:
            load.wait()
        swap_rows(0, gate_got, gate_sum, gate_rows)
        swap_rows(1, up_got, up_sum, up_rows)
        dq_sum[...] = jnp.zeros_like(dq_sum)

        def key_group(g):
            kv = side_by_side(kv_ref, g)
            keys = join(kv[:dim], ka_ref[g])
            values = join(kv[dim:], jnp.ones((dim, group), BF16))
            kv_sum[...] = jnp.zeros_like(kv_sum)
            for i in range(groups * blocks):
                q_rows = slice(i * QUERY_BLOCK, (i + 1) * QUERY_BLOCK)
                probs = jnp.exp(nn(qq_ref[q_rows, :], keys))
                score_grad = (probs * nn(dd_ref[q_rows, :], values)).astype(BF16)
                kv_sum[dim:, :] += nn(tokens_of(do_ref, i), probs.astype(BF16))
                kv_sum[:dim, :] += nn(tokens_of(q_ref, i), score_grad)
                dq_sum[q_rows, :] += nt(score_grad, keys)

        def to_pair(i):
            return copy(kv_send.at[0, i], kv_other.at[i], pair_sent.at[i], pair_got.at[i], (s, flipped(f, 0)))

        def to_owner(i):
            to = lax.rem(f + 2 * (i + 1), F)
            return copy(kv_send.at[1, i], dkvs.at[f // 2], dkv_sent.at[i], dkv_got.at[i], (s, to))

        def others(i, _):
            key_group(lax.rem(flipped(f, 0) + 2 * (i + 1), F))
            kv_send[0, i] = kv_sum[...].astype(BF16)
            to_pair(i).start()
            return 0

        lax.fori_loop(0, half, others, 0)
        layer.step(1)
        here, sends = spreads[0]
        here.wait()
        for send in sends:
            send.wait_recv()
        swap_rows(2, out_got, out_sum, out_rows)

        def owns(i, _):
            key_group(lax.rem(f + 2 * (i + 1), F))
            to_pair(i).wait_recv()
            kv_send[1, i] = (kv_sum[...] + kv_other[i].astype(F32)).astype(BF16)
            pl.when(i < half - 1)(lambda: to_owner(i).start())
            layer.step(2 + i // 2, lax.rem(i, 2) == 1)
            return 0

        lax.fori_loop(0, half, owns, 0)
        dkvs[f // 2] = kv_send[1, half - 1]
        for time in range(2 + half // 2, S):
            layer.step(time)

        bias_ref[...] = jnp.zeros_like(bias_ref)

        def dq_copy(d):
            to = lax.rem(f + d * splits, F)
            return copy(dq_send.at[to // splits], dqs.at[column], dq_sent.at[d], dq_got.at[d], (s, to))

        def queries_done(i, _):
            j, cols = i // blocks, rows_at(i % blocks)
            dq_t = dq_sum[rows_at(i), :].T
            dq_send[j, :, cols] = (dq_t[:dim] * dim**-0.5).astype(BF16)
            by_variate = dq_t[dim : dim + VARIATES]
            bias_ref[0] += by_variate * qa_ref[j, VAR_ROW : VAR_ROW + VARIATES, cols].astype(F32)
            bias_ref[1] += by_variate
            return 0

        lax.fori_loop(0, groups * blocks, queries_done, 0)
        for d in range(1, groups):
            dq_copy(d).start()
        dqs[column] = dq_send[column]
        here, sends = spreads[1]
        here.wait()
        for send in sends:
            send.wait_recv()
        to_plane = lax.rem(lax.rem(f, S) - s + S, S)
        down_sum[...] = jnp.sum(down_got[...].astype(F32), axis=0).astype(BF16)
        down_move = copy(down_sum, down_moved, down_sent, down_arrived, (to_plane, f))
        pl.when(to_plane != s)(down_move.start)

        @pl.when(to_plane == s)
        def _():
            down_moved[...] = down_sum[...]

        same = jnp.sum(bias_ref[0], keepdims=True)
        other = jnp.sum(bias_ref[1], keepdims=True) - same
        mine = lax.broadcasted_iota(jnp.int32, (1, 128), 1) == s * own_heads + column
        bias_tile = jnp.concatenate([jnp.where(mine, same, 0.0), jnp.where(mine, other, 0.0)])
        layer_own[...] = layer_ref[s]

        for load in loads[3:]:
            load.wait()
        for d in range(1, groups):
            dq_copy(d).wait_recv()
        for i in range(half - 1):
            to_owner(i).wait_recv()

        cosine, sine = cos_ref[...], sin_ref[...]
        gain_q, gain_k = [
            jnp.broadcast_to(ref[...], (128, dim)).T[:, :1] for ref in (gain_q_ref, gain_k_ref)
        ]

        def prepare_back(grad, raw, gain):
            front, back = grad[: dim // 2], grad[dim // 2 :]
            grad = join(front * cosine + back * sine, back * cosine - front * sine)
            inverse = lax.rsqrt(jnp.mean(raw * raw, axis=0, keepdims=True) + EPSILON)
            scaled = grad * gain
            mean = jnp.mean(scaled * raw, axis=0, keepdims=True)
            return inverse * scaled - raw * (inverse**3 * mean), grad * raw * inverse

        def gain_row(terms):
            folded = terms[:, :128]
            for n in range(1, group // 128):
                folded = folded + terms[:, n * 128 : (n + 1) * 128]
            return jnp.sum(folded.T, axis=0, keepdims=True)

        gain_terms = [jnp.zeros((dim, group), F32), jnp.zeros((dim, group), F32)]
        for h in range(own_heads):
            kv_grad = dkvs[h * (splits // 2)].astype(F32)
            for n in range(1, splits // 2):
                kv_grad = kv_grad + dkvs[h * (splits // 2) + n].astype(F32)
            kv_grad = kv_grad.astype(BF16).astype(F32)
            for n, (grad, gain) in enumerate(((dqs[h].astype(F32), gain_q), (kv_grad[:dim], gain_k))):
                back, terms = prepare_back(grad, raw_ref[n, h], gain)
                gain_terms[n] += terms
                pg_ref[:, pl.ds(n * lanes + h * dim, dim)] = back.T.astype(BF16)
            pg_ref[:, pl.ds(2 * lanes + h * dim, dim)] = kv_grad[dim:].T.astype(BF16)

        attn_gain = jnp.zeros((1, width), F32)
        for b in range(S):
            grad = nt(pg_ref[pl.ds(b * rows, rows), :], ws_ref[...])
            x = xs_ref[b].astype(F32)
            inverse = lax.rsqrt(jnp.mean(x * x, axis=1, keepdims=True) + EPSILON)
            attn_gain += jnp.sum(grad * x * inverse, axis=0, keepdims=True)
            u_ref[b] = grad.astype(BF16)
        normed_sum = LineSum(u_ref, from_left, from_right, (u_sent, u_got), s, f, S)
        normed_sum.step(0)

        for b in range(S):
            normed = rms_scale(xs_ref[b].astype(F32), gain_ref[...]).astype(BF16)
            terms = tn(normed, pg_ref[pl.ds(b * rows, rows), :])
            w_terms = terms if b == 0 else w_terms + terms
        w_part[...] = w_terms.astype(BF16).reshape(S, F, cut, 3 * lanes)
        w_got[f] = w_part[:, f]
        w_sends = []
        for d in range(1, F):
            to = lax.rem(f + d, F)
            w_sends.append(copy(w_part.at[:, to], w_got.at[f], w_sent.at[d], w_arrived.at[d], (s, to)))
            w_sends[-1].start()

        gains = jnp.concatenate([gain_row(gain_terms[0]), gain_row(gain_terms[1])], axis=1)
        gains = jnp.concatenate([gains, jnp.zeros((1, 256 - 2 * dim), F32)], axis=1)[:, :128]
        for n in range(chunks):
            lanes_ = slice(n * 128, (n + 1) * 128)
            vec[n] = jnp.concatenate(
                [attn_gain[:, lanes_], feed_ref[:, lanes_], gains, bias_tile, jnp.zeros((3, 128), F32)]
            )
        me = s * F + f
        vec_got[me] = vec[me * cut // 128]
        small = []
        for a in range(S):
            for b in range(F):
                if a or b:
                    to = (lax.rem(s + a, S), lax.rem(f + b, F))
                    chunk = (to[0] * F + to[1]) * cut // 128
                    n = a * F + b
                    small.append(copy(vec.at[chunk], vec_got.at[me], vec_sent.at[n], vec_arrived.at[n], to))
                    small[-1].start()

        for time in range(1, S - 1):
            normed_sum.step(time)
        for send in w_sends:
            send.wait_recv()
        w_sum[...] = jnp.sum(w_got[...].astype(F32), axis=0).astype(BF16)
        w_rows[s] = w_sum[s]
        last = []
        for d in range(1, S):
            to = lax.rem(s + d, S)
            last.append(copy(w_sum.at[to], w_rows.at[s], rows_sent.at[d], rows_got.at[d], (to, f)))
            last[-1].start()
        normed_sum.step(S - 1)
        u_own[...] = u_ref[s]

        for send in swaps + small + last:
            send.wait()
        for send in w_sends:
            send.wait_send()
        pl.when(to_plane != s)(down_move.wait)
        for _, sends in spreads:
            for send in sends:
                send.wait_send()
        for i in range(half):
            to_pair(i).wait_send()
            if i < half - 1:
                to_owner(i).wait_send()
        for d in range(1, groups):
            dq_copy(d).wait_send()
        layer.drain()
        normed_sum.drain()

    u_own, w_rows, gate_rows, up_rows, out_rows, down_moved, layer_own, vec_got = pl.pallas_call(
        kernel_g,
        in_specs=[VMEM] * 13 + [ANY] * 8,
        out_specs=[VMEM] * 8,
        out_shape=[
            shape((rows, width)),
            shape((S, cut, 3 * lanes)),
            shape((S, cut, hidden)),
            shape((S, cut, hidden)),
            shape((S, cut, width)),
            shape((down_rows, width)),
            shape((rows, width)),
            shape((count, small_rows, 128), F32),
        ],
        scratch_shapes=[
            pltpu.VMEM((half, S, cut, width), BF16),
            pltpu.VMEM((half, down_rows, width), BF16),
            pltpu.VMEM((half, S, cut, hidden), BF16),
            pltpu.VMEM((half, S, cut, hidden), BF16),
            *[pltpu.VMEM((groups * group, 2 * dim), BF16)] * 2,
            pltpu.VMEM((groups * group, 2 * dim), F32),
            pltpu.VMEM((2 * dim, group), F32),
            pltpu.VMEM((2, half, 2 * dim, group), BF16),
            pltpu.VMEM((half, 2 * dim, group), BF16),
            pltpu.VMEM((groups, dim, group), BF16),
            pltpu.VMEM((own_heads, dim, group), BF16),
            pltpu.VMEM((half, 2 * dim, group), BF16),
            pltpu.VMEM((S, cut, hidden), BF16),
            pltpu.VMEM((S, cut, hidden), BF16),
            pltpu.VMEM((S, cut, width), BF16),
            pltpu.VMEM((down_rows, width), BF16),
            *[pltpu.VMEM((S, rows, width), BF16)] * 3,
            pltpu.VMEM((2, own_heads, dim, group), F32),
            pltpu.VMEM((width, 3 * lanes), BF16),
            pltpu.VMEM((S, rows, width), BF16),
            pltpu.VMEM((group, 3 * lanes), BF16),
            *[pltpu.VMEM((S, rows, width), BF16)] * 3,
            pltpu.VMEM((S, F, cut, 3 * lanes), BF16),
            pltpu.VMEM((F, S, cut, 3 * lanes), BF16),
            pltpu.VMEM((S, cut, 3 * lanes), BF16),
            pltpu.VMEM((chunks, small_rows, 128), F32),
            pltpu.VMEM((2, VARIATES, QUERY_BLOCK), F32),
            dma((6,)),
            dma((2,)),
            *[dma((2, half))] * 2,
            *[dma((2, S))] * 2,
            *[dma((3, S))] * 2,
            *[dma((half,))] * 2,
            *[dma((half,))] * 2,
            *[dma((groups,))] * 2,
            *[dma((2, S))] * 2,
            *[dma((F,))] * 2,
            *[dma((S,))] * 2,
            *[dma((count,))] * 2,
            dma,
            dma,
        ],
        compiler_params=pltpu.CompilerParams(
            collective_id=1, has_side_effects=True, vmem_limit_bytes=VMEM_BYTES
        ),
    )(
        q_all, kv_all, query_marks, key_marks, grad_heads, attended, log_sum, cosine, sine, gain_query[None, :],
        gain_key[None, :], feed_gain, gain_attn[None, :], output_half, down_half, out_part, gate_got, up_got, raw, w_qkv,
        x_parts,
    )

    def kernel_z(
        x_ref, middle_ref, mid_grad_ref, u_ref, w_ref, gate_rows, up_rows, out_rows, down_ref, layer_ref, vec_ref, gain_ref,
        layer_out, tokens_out, attn_out, output_out, gate_out, up_out, down_out, attn_gain, feed_gain, gain_q, gain_k, bias,
    ):
        s, f = lax.axis_index("seq"), lax.axis_index("fsdp")
        layer_out[...] = (middle_ref[...] + layer_ref[...].astype(F32)).astype(BF16)
        x, grad = x_ref[...].astype(F32), u_ref[...].astype(F32)
        inverse = lax.rsqrt(jnp.mean(x * x, axis=1, keepdims=True) + EPSILON)
        scaled = grad * gain_ref[...]
        mean = jnp.mean(scaled * x, axis=1, keepdims=True)
        tokens_out[...] = mid_grad_ref[...] + inverse * scaled - x * (inverse**3 * mean)
        for n in range(S):
            for part in range(3):
                place = part * S * lanes + n * lanes
                attn_out[:, place : place + lanes] = w_ref[n, :, part * lanes : (part + 1) * lanes].astype(F32)
            for g in range(F):
                holder = (g % S - n) % S * per_plane + g // S
                place = (holder * S + g % S) * down_rows
                cols = slice(g * down_rows, (g + 1) * down_rows)
                gate_out[:, place : place + down_rows] = gate_rows[n, :, cols].astype(F32)
                up_out[:, place : place + down_rows] = up_rows[n, :, cols].astype(F32)
        output_out[...] = jnp.sum(out_rows[...].astype(F32), axis=0)
        down_out[...] = down_ref[...].astype(F32)
        sums = jnp.sum(vec_ref[...], axis=0)
        place = lax.rem((s * F + f) * cut, 128)
        for row, ref in ((0, attn_gain), (1, feed_gain)):
            picked = jnp.zeros((1, cut), F32)
            for n in range(0, 128, cut):
                picked = picked + jnp.where(place == n, sums[row : row + 1, n : n + cut], 0.0)
            ref[...] = picked
        gain_q[...] = sums[2:3, :dim]
        gain_k[...] = sums[2:3, dim : 2 * dim]
        bias[...] = sums[3:5, :heads]

    out = pl.pallas_call(
        kernel_z,
        in_specs=[VMEM] * 12,
        out_specs=[VMEM] * 12,
        out_shape=[
            shape((rows, width)),
            shape((rows, width), F32),
            shape((cut, 3 * S * lanes), F32),
            shape((cut, width), F32),
            shape((cut, S * hidden), F32),
            shape((cut, S * hidden), F32),
            shape((down_rows, width), F32),
            shape((1, cut), F32),
            shape((1, cut), F32),
            shape((1, dim), F32),
            shape((1, dim), F32),
            shape((2, heads), F32),
        ],
        compiler_params=pltpu.CompilerParams(vmem_limit_bytes=VMEM_BYTES),
    )(
        tokens, own_middle, middle_grad, u_own, w_rows, gate_rows, up_rows, out_rows, down_moved, layer_own, vec_got,
        gain_attn[None, :],
    )
    return (*out[:7], *[row[0] for row in out[7:11]], out[11].T)


def solution(mesh):
    by_token, by_fsdp, by_owner = P(("fsdp", "seq"), None), P("fsdp", None), P(("seq", "fsdp"), None)
    in_specs = (
        by_token,
        by_token,
        P(),
        P(),
        P(),
        P(),
        by_fsdp,
        P(),
        P(),
        P(),
        by_fsdp,
        P(),
        by_fsdp,
        by_fsdp,
        by_fsdp,
    )
    out_specs = (
        (by_token, by_token) + (by_owner,) * 5 + (P(("seq", "fsdp")),) * 2 + (P(),) * 3
    )
    return jax.shard_map(
        per_device, mesh=mesh, in_specs=in_specs, out_specs=out_specs, check_vma=False
    )
```

time: 257 us -> 206 us (0.80)
  the two profiles are of different devices: /device:TPU:0 before, /device:TPU:1 now
where the time goes in v1:
time: 206 us; the launch traced here: 202 us
  Pallas kernels  201 us (98%)
    pallas_call x1, Pallas kernels, per_device(): pl.pallas_call(kernel_a, in_specs=[VMEM] * 2 + [ANY] * 5 + [VMEM] * 8 + [...  123 us
    pallas_call x1, Pallas kernels, per_device(): pl.pallas_call(kernel_g, in_specs=[VMEM] * 13 + [ANY] * 8, out_specs=[VME...  74 us

profile of v1, /device:TPU:1, one launch (start us, length us, event | category | flops | bytes accessed | tf_op | source)
XLA Modules:
  0.0 202.3 jit_solution(3414238313325544857)
XLA Ops:
  0.6 0.6 multiply_power_fusion.freq_ref
  1.3 122.9 %shard_map.238 = (bf16[4,128,1024]{2,1,0:T(8,128)(2,1)}, bf16[1024,768]{1,0:T(8,128)(2,1)}, f32[2,4,64,512]{3,2,1,0:T(8,128)}, f32[32,512]{1,0:T(8,128)}, f32[32...) custom-call(bf16[128,1024]{1,0:T(8,128)(2,1)} %x_ref.3, ...), custom_call_target="tpu_custom_call" | custom-call | flops 20000000000 | bytes 100000000 | tf_op jit(solution)/shard_map/pallas_call | solution.py:826
  124.2 74.0 %shard_map.239 = (bf16[128,1024]{1,0:T(8,128)(2,1)}, bf16[4,32,768]{2,1,0:T(8,128)(2,1)}, bf16[4,32,1024]{2,1,0:T(8,128)(2,1)}, bf16[4,32,1024]{2,1,0:T(8,128)(2...) custom-call(bf16[4,4,64,128]{3,2,1,0:T(8,128)(2,1)} %get-tuple-eleme, ...), custom_call_target="tpu_custom_call" | custom-call | tf_op jit(solution)/shard_map/pallas_call | solution.py:1202
  198.2 3.7 %shard_map.240 = (bf16[128,1024]{1,0:T(8,128)(2,1)}, f32[128,1024]{1,0:T(8,128)}, f32[32,3072]{1,0:T(8,128)}, f32[32,1024]{1,0:T(8,128)}, f32[32,4096]{1,0:T(8,1...) custom-call(bf16[128,1024]{1,0:T(8,128)(2,1)} %x_ref.3, ...), custom_call_target="tpu_custom_call" | custom-call | tf_op jit(solution)/shard_map/pallas_call | solution.py:1302

commit v2 on v1

--- a/solution.py
+++ b/solution.py
@@ -113,6 +113,27 @@
         pl.when(s + distance < S)(lambda: self.hop(s + distance, slot, -1).wait_recv())
         self.each_hop(slot, distance, lambda hop: hop.start())
 
+    def follow(self, slot, time):
+        s, S = self.s, self.S
+        p = 2 * s + 1 - time
+        now = (p >= 0) & (p <= s) & (s + 1 < S)
+        pl.when(now & (p < s))(lambda: self.hop(p, slot, 1).wait_recv())
+        pl.when(now)(lambda: self.hop(p, slot, 1).start())
+        m = S - 1 - s
+        q = 2 * m + 1 - time
+        now = (q >= 0) & (q <= m) & (s >= 1)
+        pl.when(now & (q < m))(lambda: self.hop(S - 1 - q, slot, -1).wait_recv())
+        pl.when(now)(lambda: self.hop(S - 1 - q, slot, -1).start())
+
+    def follow_end(self, slot):
+        for distance in range(1, self.S):
+            pl.when(self.s == self.S - 1)(
+                lambda distance=distance: self.hop(self.s - distance, slot, 1).wait_recv()
+            )
+            pl.when(self.s == 0)(
+                lambda distance=distance: self.hop(self.s + distance, slot, -1).wait_recv()
+            )
+
     def drain(self, slot):
         for distance in range(self.S):
             self.each_hop(slot, distance, lambda hop: hop.wait_send())
@@ -158,6 +179,23 @@
         for t in range(self.S):
             pl.when(self.s < t)(lambda t=t: self.hop(t, True).wait_send())
             pl.when(self.s > t)(lambda t=t: self.hop(t, False).wait_send())
+
+
+class LineSums:
+    def __init__(self, terms, from_left, from_right, sems, s, f, S):
+        size = terms.shape[1] // 2
+        self.parts = []
+        for n in range(2):
+            refs = [ref.at[:, pl.ds(n * size, size)] for ref in (terms, from_left, from_right)]
+            self.parts.append(LineSum(*refs, sems[2 * n : 2 * n + 2], s, f, S))
+
+    def step(self, time, now=True):
+        for part in self.parts:
+            part.step(time, now)
+
+    def drain(self):
+        for part in self.parts:
+            part.drain()
 
 
 def flipped(f, bit):
@@ -411,7 +449,7 @@
         xs_ref, ws_ref, raw_ref, cots_ref, ka_ref, qa_ref, q_ref, kv_ref, att_ref, heads_ref, wos_ref, gates_ref, ups_ref,
         downs_ref, mid_v, n_v, n_t, hid_v, hid_t, gl_v, ul_v, u_ref, from_left, from_right,
         gate_part, up_part, down_part, output_part, gate_other, up_other, down_other, output_other, gate_half, up_half,
-        hg_ref, u_sent, u_got, pair_sent, pair_got, spread_sent, spread_got, own_sem, f_sent, f_got, out_sem,
+        hg_ref, u_sent, u_got, u_sent_, u_got_, pair_sent, pair_got, spread_sent, spread_got, own_sem, f_sent, f_got, out_sem,
         q_out, kv_out, o_ref, gate_own, up_own,
         w_sem, unit_sem, here_sem, x_sent, x_got, c_sent, c_got, kv_sent, kv_shared, kv_got, q_sent, q_got,
         o_sent, h_sent, h_got, *cube_refs,
@@ -559,26 +597,29 @@
                 to_neighbour(b, d).wait_recv()
                 to_neighbour(b, d).start()
 
-        for number in range(1, ws.rounds + 1):
+        wos.start()
+        gates.start()
+        ws.step(1)
+        wos.step(1)
+        gates.step(1)
+        for number in range(2, ws.rounds + 1):
             ws.step(number)
-        wos.start()
         ws.finish()
         project(s)
         for distance in range(1, S):
             xs.arrive(0, distance)
-            if distance == S - 1:
-                cots.send(0)
+            cots.follow(0, distance)
             pl.when(s - distance >= 0)(lambda distance=distance: project(s - distance))
             pl.when(s + distance < S)(lambda distance=distance: project(s + distance))
-            if distance == S - 2:
-                wos.step(1)
 
         def share_all(b, _):
             share(b)
             return 0
 
-        lax.fori_loop(0, S, share_all, 0)
-        gates.start()
+        for time in range(S, 2 * S - 2):
+            if time == (3 * S - 2) // 2:
+                lax.fori_loop(0, S, share_all, 0)
+            cots.follow(0, time)
 
         def last(b, _):
             for d in range(half):
@@ -626,19 +667,13 @@
                     to_column(came).wait_recv()
                 for d in range(1, S):
                     along(came, d).start()
-            if turn + 1 < S:
-                cots.arrive(0, turn + 1)
             if turn == 0:
-                gates.step(1)
-            if turn == 2:
                 for number in range(2, wos.rounds + 1):
                     wos.step(number)
                     gates.step(number)
             if turn == 3:
                 ups.step(1)
                 downs.step(1)
-        for distance in range(groups + 2, S):
-            cots.arrive(0, distance)
         for number in range(2, ups.rounds + 1):
             ups.step(number)
             downs.step(number)
@@ -659,6 +694,7 @@
                 along(turn, d).wait_recv()
         for copy_ in here:
             copy_.wait()
+        cots.follow_end(0)
         wos.finish()
 
         def copy(src, dst, sent, got, to):
@@ -691,7 +727,8 @@
             cs = slice(c, c + block)
             grad = nt(gl_v[...], gates_ref[cs, :]) + nt(ul_v[...], ups_ref[cs, :])
             u_ref[:, :, cs] = grad.astype(BF16).reshape(S, rows, block)
-        mid_sum = LineSum(u_ref, from_left, from_right, (u_sent, u_got), s, f, S)
+        u_sems = (u_sent, u_got, u_sent_, u_got_)
+        mid_sum = LineSums(u_ref, from_left, from_right, u_sems, s, f, S)
         mid_sum.step(0)
 
         parity = lax.rem(f, 2)
@@ -868,7 +905,7 @@
             pltpu.VMEM((S, half, cut, width), BF16),
             *[pltpu.VMEM(wide_half, BF16)] * 2,
             pltpu.VMEM((heads, dim, rows), BF16),
-            *[dma((2, S))] * 2,
+            *[dma((2, S))] * 4,
             *[dma((4,))] * 2,
             *[dma((2, half))] * 2,
             dma((3,)),
@@ -917,7 +954,6 @@
         doc_starts,
     )
 
-    count = S * F
     chunks = width // 128
     blocks = group // QUERY_BLOCK
     span = QUERY_BLOCK // rows
@@ -929,10 +965,10 @@
         u_own, w_rows, gate_rows, up_rows, out_rows, down_moved, layer_own, vec_got,
         out_got, down_got, gate_got, up_got,
         qq_ref, dd_ref, dq_sum, kv_sum, kv_send, kv_other, dq_send, dqs, dkvs, gate_sum, up_sum, out_sum, down_sum,
-        layer_ref, layer_left, layer_right, raw_ref, ws_ref, xs_ref, pg_ref, u_ref, from_left, from_right, w_part, w_got,
-        w_sum, vec, bias_ref,
+        layer_ref, layer_left, layer_right, raw_ref, ws_ref, xs_ref, pg_ref, u_ref, from_left, from_right, w_part, w_other,
+        w_half, w_got, w_sum, vec, normed_t, bias_ref,
         load_sem, own_sem, spread_sent, spread_got, layer_sent, layer_got, swap_sent, swap_got, pair_sent, pair_got,
-        dkv_sent, dkv_got, dq_sent, dq_got, u_sent, u_got, w_sent, w_arrived, rows_sent, rows_got, vec_sent, vec_arrived,
+        dkv_sent, dkv_got, dq_sent, dq_got, u_sent, u_got, u_sent_, u_got_, half_sent, half_got, w_sent, w_arrived, rows_sent, rows_got, vec_sent, vec_arrived,
         down_sent, down_arrived,
     ):
         s, f = lax.axis_index("seq"), lax.axis_index("fsdp")
@@ -979,6 +1015,11 @@
                 swaps.append(copy(total.at[to], rows_ref.at[s], swap_sent.at[n, d], swap_got.at[n, d], (to, f)))
                 swaps[-1].start()
 
+        for load in loads[1:3]:
+            load.wait()
+        swap_rows(0, gate_got, gate_sum, gate_rows)
+        swap_rows(1, up_got, up_sum, up_rows)
+
         def rows_at(i):
             return pl.ds(pl.multiple_of(i * QUERY_BLOCK, QUERY_BLOCK), QUERY_BLOCK)
 
@@ -998,10 +1039,6 @@
             return 0
 
         lax.fori_loop(0, groups * blocks, ready, 0)
-        for load in loads[1:3]:
-            load.wait()
-        swap_rows(0, gate_got, gate_sum, gate_rows)
-        swap_rows(1, up_got, up_sum, up_rows)
         dq_sum[...] = jnp.zeros_like(dq_sum)
 
         def key_group(g):
@@ -1043,13 +1080,11 @@
             to_pair(i).wait_recv()
             kv_send[1, i] = (kv_sum[...] + kv_other[i].astype(F32)).astype(BF16)
             pl.when(i < half - 1)(lambda: to_owner(i).start())
-            layer.step(2 + i // 2, lax.rem(i, 2) == 1)
             return 0
 
         lax.fori_loop(0, half, owns, 0)
         dkvs[f // 2] = kv_send[1, half - 1]
-        for time in range(2 + half // 2, S):
-            layer.step(time)
+        layer.step(2)
 
         bias_ref[...] = jnp.zeros_like(bias_ref)
 
@@ -1087,12 +1122,15 @@
         other = jnp.sum(bias_ref[1], keepdims=True) - same
         mine = lax.broadcasted_iota(jnp.int32, (1, 128), 1) == s * own_heads + column
         bias_tile = jnp.concatenate([jnp.where(mine, same, 0.0), jnp.where(mine, other, 0.0)])
-        layer_own[...] = layer_ref[s]
 
         for load in loads[3:]:
             load.wait()
-        for d in range(1, groups):
-            dq_copy(d).wait_recv()
+        for time in range(3, S):
+            layer.step(time)
+        layer_own[...] = layer_ref[s]
+        x = xs_ref[...].astype(F32).reshape(group, width)
+        inverse = lax.rsqrt(jnp.mean(x * x, axis=1, keepdims=True) + EPSILON)
+        normed_t[...] = (x * inverse * gain_ref[...]).astype(BF16).T
         for i in range(half - 1):
             to_owner(i).wait_recv()
 
@@ -1115,41 +1153,43 @@
                 folded = folded + terms[:, n * 128 : (n + 1) * 128]
             return jnp.sum(folded.T, axis=0, keepdims=True)
 
-        gain_terms = [jnp.zeros((dim, group), F32), jnp.zeros((dim, group), F32)]
+        key_terms = jnp.zeros((dim, group), F32)
         for h in range(own_heads):
             kv_grad = dkvs[h * (splits // 2)].astype(F32)
             for n in range(1, splits // 2):
                 kv_grad = kv_grad + dkvs[h * (splits // 2) + n].astype(F32)
             kv_grad = kv_grad.astype(BF16).astype(F32)
-            for n, (grad, gain) in enumerate(((dqs[h].astype(F32), gain_q), (kv_grad[:dim], gain_k))):
-                back, terms = prepare_back(grad, raw_ref[n, h], gain)
-                gain_terms[n] += terms
-                pg_ref[:, pl.ds(n * lanes + h * dim, dim)] = back.T.astype(BF16)
+            back, terms = prepare_back(kv_grad[:dim], raw_ref[1, h], gain_k)
+            key_terms += terms
+            pg_ref[:, pl.ds(lanes + h * dim, dim)] = back.T.astype(BF16)
             pg_ref[:, pl.ds(2 * lanes + h * dim, dim)] = kv_grad[dim:].T.astype(BF16)
-
-        attn_gain = jnp.zeros((1, width), F32)
-        for b in range(S):
-            grad = nt(pg_ref[pl.ds(b * rows, rows), :], ws_ref[...])
-            x = xs_ref[b].astype(F32)
-            inverse = lax.rsqrt(jnp.mean(x * x, axis=1, keepdims=True) + EPSILON)
-            attn_gain += jnp.sum(grad * x * inverse, axis=0, keepdims=True)
-            u_ref[b] = grad.astype(BF16)
-        normed_sum = LineSum(u_ref, from_left, from_right, (u_sent, u_got), s, f, S)
+        for d in range(1, groups):
+            dq_copy(d).wait_recv()
+        query_terms = jnp.zeros((dim, group), F32)
+        for h in range(own_heads):
+            back, terms = prepare_back(dqs[h].astype(F32), raw_ref[0, h], gain_q)
+            query_terms += terms
+            pg_ref[:, pl.ds(h * dim, dim)] = back.T.astype(BF16)
+
+        attn_gain = []
+        for c in range(0, width, block):
+            cs = slice(c, c + block)
+            grad = nt(pg_ref[...], ws_ref[cs, :])
+            scaled = xs_ref[:, :, cs].astype(F32).reshape(group, block) * inverse
+            attn_gain.append(jnp.sum(grad * scaled, axis=0, keepdims=True))
+            u_ref[:, :, cs] = grad.astype(BF16).reshape(S, rows, block)
+        attn_gain = jnp.concatenate(attn_gain, axis=1)
+        normed_sum = LineSums(u_ref, from_left, from_right, (u_sent, u_got, u_sent_, u_got_), s, f, S)
         normed_sum.step(0)
 
-        for b in range(S):
-            normed = rms_scale(xs_ref[b].astype(F32), gain_ref[...]).astype(BF16)
-            terms = tn(normed, pg_ref[pl.ds(b * rows, rows), :])
-            w_terms = terms if b == 0 else w_terms + terms
-        w_part[...] = w_terms.astype(BF16).reshape(S, F, cut, 3 * lanes)
-        w_got[f] = w_part[:, f]
-        w_sends = []
-        for d in range(1, F):
-            to = lax.rem(f + d, F)
-            w_sends.append(copy(w_part.at[:, to], w_got.at[f], w_sent.at[d], w_arrived.at[d], (s, to)))
-            w_sends[-1].start()
-
-        gains = jnp.concatenate([gain_row(gain_terms[0]), gain_row(gain_terms[1])], axis=1)
+        step = 256 if 3 * lanes % 256 == 0 else 128
+        for c in range(0, 3 * lanes, step):
+            cs = slice(c, c + step)
+            terms = nn(normed_t[...], pg_ref[:, cs]).astype(BF16)
+            w_part[..., cs] = terms.reshape(S, half, 2, cut, step)
+        to_other = copy(w_part.at[:, :, 1 - parity], w_other, half_sent, half_got, (s, flipped(f, 0)))
+        to_other.start()
+        gains = jnp.concatenate([gain_row(query_terms), gain_row(key_terms)], axis=1)
         gains = jnp.concatenate([gains, jnp.zeros((1, 256 - 2 * dim), F32)], axis=1)[:, :128]
         for n in range(chunks):
             lanes_ = slice(n * 128, (n + 1) * 128)
@@ -1159,15 +1199,18 @@
         me = s * F + f
         vec_got[me] = vec[me * cut // 128]
         small = []
-        for a in range(S):
-            for b in range(F):
-                if a or b:
-                    to = (lax.rem(s + a, S), lax.rem(f + b, F))
-                    chunk = (to[0] * F + to[1]) * cut // 128
-                    n = a * F + b
-                    small.append(copy(vec.at[chunk], vec_got.at[me], vec_sent.at[n], vec_arrived.at[n], to))
-                    small[-1].start()
-
+        for n, to in enumerate(everyone(s, f)):
+            chunk = (to[0] * F + to[1]) * cut // 128
+            small.append(copy(vec.at[chunk], vec_got.at[me], vec_sent.at[n], vec_arrived.at[n], to))
+            small[-1].start()
+
+        to_other.wait()
+        w_half[...] = (w_part[:, :, parity].astype(F32) + w_other[...].astype(F32)).astype(BF16)
+        w_got[f // 2] = w_half[:, f // 2]
+        w_sends = []
+        for d, to in enumerate(same_parity(s, f)):
+            w_sends.append(copy(w_half.at[:, to[1] // 2], w_got.at[f // 2], w_sent.at[d], w_arrived.at[d], to))
+            w_sends[-1].start()
         for time in range(1, S - 1):
             normed_sum.step(time)
         for send in w_sends:
@@ -1211,7 +1254,7 @@
             shape((S, cut, width)),
             shape((down_rows, width)),
             shape((rows, width)),
-            shape((count, small_rows, 128), F32),
+            shape((S * F, small_rows, 128), F32),
         ],
         scratch_shapes=[
             pltpu.VMEM((half, S, cut, width), BF16),
@@ -1236,10 +1279,13 @@
             pltpu.VMEM((S, rows, width), BF16),
             pltpu.VMEM((group, 3 * lanes), BF16),
             *[pltpu.VMEM((S, rows, width), BF16)] * 3,
-            pltpu.VMEM((S, F, cut, 3 * lanes), BF16),
-            pltpu.VMEM((F, S, cut, 3 * lanes), BF16),
+            pltpu.VMEM((S, half, 2, cut, 3 * lanes), BF16),
+            pltpu.VMEM((S, half, cut, 3 * lanes), BF16),
+            pltpu.VMEM((S, half, cut, 3 * lanes), BF16),
+            pltpu.VMEM((half, S, cut, 3 * lanes), BF16),
             pltpu.VMEM((S, cut, 3 * lanes), BF16),
             pltpu.VMEM((chunks, small_rows, 128), F32),
+            pltpu.VMEM((width, group), BF16),
             pltpu.VMEM((2, VARIATES, QUERY_BLOCK), F32),
             dma((6,)),
             dma((2,)),
@@ -1249,10 +1295,12 @@
             *[dma((half,))] * 2,
             *[dma((half,))] * 2,
             *[dma((groups,))] * 2,
-            *[dma((2, S))] * 2,
-            *[dma((F,))] * 2,
+            *[dma((2, S))] * 4,
+            dma,
+            dma,
+            *[dma((half,))] * 2,
             *[dma((S,))] * 2,
-            *[dma((count,))] * 2,
+            *[dma((S * F,))] * 2,
             dma,
             dma,
         ],

time: 206 us -> 199 us (0.966)
  the two profiles are of different devices: /device:TPU:1 before, /device:TPU:0 now
where the time goes in v2:
time: 199 us; the launch traced here: 195 us
  Pallas kernels  194 us (97%)
    pallas_call x1, Pallas kernels, per_device(): pl.pallas_call(kernel_a, in_specs=[VMEM] * 2 + [ANY] * 5 + [VMEM] * 8 + [...  119 us
    pallas_call x1, Pallas kernels, per_device(): pl.pallas_call(kernel_g, in_specs=[VMEM] * 13 + [ANY] * 8, out_specs=[VME...  71.1 us

profile of v2, /device:TPU:0, one launch (start us, length us, event | category | flops | bytes accessed | tf_op | source)
XLA Modules:
  0.0 195.3 jit_solution(4631748062968260111)
XLA Ops:
  0.6 0.6 multiply_power_fusion.freq_ref
  1.3 118.8 %shard_map.238 = (bf16[4,128,1024]{2,1,0:T(8,128)(2,1)}, bf16[1024,768]{1,0:T(8,128)(2,1)}, f32[2,4,64,512]{3,2,1,0:T(8,128)}, f32[32,512]{1,0:T(8,128)}, f32[32...) custom-call(bf16[128,1024]{1,0:T(8,128)(2,1)} %x_ref.3, ...), custom_call_target="tpu_custom_call" | custom-call | flops 20000000000 | bytes 100000000 | tf_op jit(solution)/shard_map/pallas_call | solution.py:863
  120.1 71.1 %shard_map.239 = (bf16[128,1024]{1,0:T(8,128)(2,1)}, bf16[4,32,768]{2,1,0:T(8,128)(2,1)}, bf16[4,32,1024]{2,1,0:T(8,128)(2,1)}, bf16[4,32,1024]{2,1,0:T(8,128)(2...) custom-call(bf16[4,4,64,128]{3,2,1,0:T(8,128)(2,1)} %get-tuple-eleme, ...), custom_call_target="tpu_custom_call" | custom-call | tf_op jit(solution)/shard_map/pallas_call | solution.py:1245
  191.2 3.7 %shard_map.240 = (bf16[128,1024]{1,0:T(8,128)(2,1)}, f32[128,1024]{1,0:T(8,128)}, f32[32,3072]{1,0:T(8,128)}, f32[32,1024]{1,0:T(8,128)}, f32[32,4096]{1,0:T(8,1...) custom-call(bf16[128,1024]{1,0:T(8,128)(2,1)} %x_ref.3, ...), custom_call_target="tpu_custom_call" | custom-call | tf_op jit(solution)/shard_map/pallas_call | solution.py:1350

commit v3 on v2

--- a/solution.py
+++ b/solution.py
@@ -445,11 +445,11 @@
         x_ref, cot_ref, w_ref, wo_ref, wd_ref, wg_ref, wu_ref, times_ref, ids_ref, freq_ref, gain_ref, gain_q_ref, gain_k_ref,
         gain_feed_ref, bias_ref, starts_ref,
         xs_out, ws_out, raw_out, cos_ref, sin_ref, ka_out, qa_out, qs_out, kvs_out, att_out, lse_ref,
-        grads_ref, middle_ref, mid_grad_ref, feed_ref, out_ref, gate_got, up_got, down_half, output_half,
+        grads_ref, middle_ref, mid_grad_ref, feed_ref, out_hbm, gate_got, up_got, down_hbm, output_half,
         xs_ref, ws_ref, raw_ref, cots_ref, ka_ref, qa_ref, q_ref, kv_ref, att_ref, heads_ref, wos_ref, gates_ref, ups_ref,
         downs_ref, mid_v, n_v, n_t, hid_v, hid_t, gl_v, ul_v, u_ref, from_left, from_right,
         gate_part, up_part, down_part, output_part, gate_other, up_other, down_other, output_other, gate_half, up_half,
-        hg_ref, u_sent, u_got, u_sent_, u_got_, pair_sent, pair_got, spread_sent, spread_got, own_sem, f_sent, f_got, out_sem,
+        hg_ref, out_ref, down_half, u_sent, u_got, u_sent_, u_got_, pair_sent, pair_got, spread_sent, spread_got, own_sem, f_sent, f_got, out_sem,
         q_out, kv_out, o_ref, gate_own, up_own,
         w_sem, unit_sem, here_sem, x_sent, x_got, c_sent, c_got, kv_sent, kv_shared, kv_got, q_sent, q_got,
         o_sent, h_sent, h_got, *cube_refs,
@@ -778,6 +778,9 @@
         spreads.append(spread(1, up_half, up_got))
         swaps[2].wait_recv()
         down_half[...] = add(down_part[:, parity], down_other[...])
+        for src, dst in ((out_ref, out_hbm), (down_half, down_hbm)):
+            flushes.append(pltpu.make_async_copy(src, dst, out_sem.at[len(flushes)]))
+            flushes[-1].start()
         for time in range(2, S):
             mid_sum.step(time)
 
@@ -863,7 +866,7 @@
     ) = pl.pallas_call(
         kernel_a,
         in_specs=[VMEM] * 2 + [ANY] * 5 + [VMEM] * 8 + [pl.BlockSpec(memory_space=pltpu.SMEM)],
-        out_specs=[ANY] * 3 + [VMEM] * 2 + [ANY] * 5 + [VMEM] + [ANY] + [VMEM] * 4 + [ANY] * 2 + [VMEM] * 2,
+        out_specs=[ANY] * 3 + [VMEM] * 2 + [ANY] * 5 + [VMEM] + [ANY] + [VMEM] * 3 + [ANY] * 4 + [VMEM],
         out_shape=[
             *kept[:3],
             shape((dim // 2, group), F32),
@@ -905,12 +908,14 @@
             pltpu.VMEM((S, half, cut, width), BF16),
             *[pltpu.VMEM(wide_half, BF16)] * 2,
             pltpu.VMEM((heads, dim, rows), BF16),
+            pltpu.VMEM((S, rows, width), BF16),
+            pltpu.VMEM((half, down_rows, width), BF16),
             *[dma((2, S))] * 4,
             *[dma((4,))] * 2,
             *[dma((2, half))] * 2,
             dma((3,)),
             *[dma((S * groups,))] * 2,
-            dma((len(kept),)),
+            dma((len(kept) + 2,)),
             pltpu.VMEM((S, own_heads, dim, rows), BF16),
             pltpu.VMEM((S, own_heads, 2 * dim, rows), BF16),
             pltpu.VMEM((groups, dim, group), BF16),

time: 199 us -> 198 us (level)
  no operation moved by 1% of the time
where the time goes in v3:
time: 198 us; the launch traced here: 195 us
  Pallas kernels  193 us (97%)
    pallas_call x1, Pallas kernels, per_device(): pl.pallas_call(kernel_a, in_specs=[VMEM] * 2 + [ANY] * 5 + [VMEM] * 8 + [...  118 us
    pallas_call x1, Pallas kernels, per_device(): pl.pallas_call(kernel_g, in_specs=[VMEM] * 13 + [ANY] * 8, out_specs=[VME...  71.1 us

profile of v3, /device:TPU:0, one launch (start us, length us, event | category | flops | bytes accessed | tf_op | source)
XLA Modules:
  0.0 194.6 jit_solution(8019530746207087555)
XLA Ops:
  0.6 0.6 multiply_power_fusion.freq_ref
  1.3 118.1 %shard_map.238 = (bf16[4,128,1024]{2,1,0:T(8,128)(2,1)}, bf16[1024,768]{1,0:T(8,128)(2,1)}, f32[2,4,64,512]{3,2,1,0:T(8,128)}, f32[32,512]{1,0:T(8,128)}, f32[32...) custom-call(bf16[128,1024]{1,0:T(8,128)(2,1)} %x_ref.3, ...), custom_call_target="tpu_custom_call" | custom-call | flops 20000000000 | bytes 100000000 | tf_op jit(solution)/shard_map/pallas_call | solution.py:866
  119.4 71.1 %shard_map.239 = (bf16[128,1024]{1,0:T(8,128)(2,1)}, bf16[4,32,768]{2,1,0:T(8,128)(2,1)}, bf16[4,32,1024]{2,1,0:T(8,128)(2,1)}, bf16[4,32,1024]{2,1,0:T(8,128)(2...) custom-call(bf16[4,4,64,128]{3,2,1,0:T(8,128)(2,1)} %get-tuple-eleme, ...), custom_call_target="tpu_custom_call" | custom-call | tf_op jit(solution)/shard_map/pallas_call | solution.py:1250
  190.5 3.7 %shard_map.240 = (bf16[128,1024]{1,0:T(8,128)(2,1)}, f32[128,1024]{1,0:T(8,128)}, f32[32,3072]{1,0:T(8,128)}, f32[32,1024]{1,0:T(8,128)}, f32[32,4096]{1,0:T(8,1...) custom-call(bf16[128,1024]{1,0:T(8,128)(2,1)} %x_ref.3, ...), custom_call_target="tpu_custom_call" | custom-call | tf_op jit(solution)/shard_map/pallas_call | solution.py:1355
